TPU v7x, 128 devices: a whole 4x4x4 slice. The times are simulated.
128 devices in a mesh: dp: 4 (over z), row: 4 (over y_lo, core), col: 8 (over x, y_hi).
Axes of the slice: x: 4, y: 4 (y_hi: 2, y_lo: 2; y = y_hi * 2 + y_lo), z: 4, core: 2. Of those that a mesh axis runs over, the one named last changes fastest.
Arguments:
- features: bfloat16 [4, 96, 768, 1024], P('dp', None, 'row', 'col'), may hold values from -6 to 6
- kernel: bfloat16 [8, 96, 3, 3], replicated, may hold values from -0.21875 to 0.21875
- target_amp: float32 [4, 8, 1024, 768], P('dp', None, ('row', 'col')), may hold values from 0.2 to 3
- spec_weight: float32 [8, 1024, 768], P(None, ('row', 'col')), may hold values from 0.1 to 10
Outputs:
- kernel_grad: float32 [8, 96, 3, 3], replicated
- feature_grad: bfloat16 [4, 96, 768, 1024], P('dp', None, 'row', 'col')
All inputs are finite; a program needn't handle non-finite values.
Results may differ from a plain program's by a relative error of at most 0.015.
Values may be sent and summed in bfloat16 or wider, within the bound.
A program may use at most 256 MiB of HBM per device.

v0:
```python
import math

import jax
import jax.numpy as jnp
from jax import lax
from jax.sharding import PartitionSpec as P


def extended(cells, sides, width):
    for axis, dim in sides:
        count = lax.axis_size(axis)
        ends = count - 1
        head = lax.slice_in_dim(cells, 0, width, axis=dim)
        tail = lax.slice_in_dim(cells, cells.shape[dim] - width, cells.shape[dim], axis=dim)
        cells = jnp.concatenate(
            [
                lax.ppermute(tail, axis, [(i, (i + 1) % count) for i in range(ends)]),
                cells,
                lax.ppermute(head, axis, [((i + 1) % count, i) for i in range(ends)]),
            ],
            axis=dim,
        )
    return cells


def dft_tables(length):
    index = jnp.arange(length, dtype=jnp.int32)
    product = index[:, None] * index[None, :] % length
    angles = product.astype(jnp.float32) * (2.0 * math.pi / length)
    factor = 1.0 / math.sqrt(length)
    return (
        (jnp.cos(angles) * factor).astype(jnp.bfloat16),
        (jnp.sin(angles) * factor).astype(jnp.bfloat16),
    )


def per_device(features, kernel, target_amp, spec_weight):
    samples, chans, rows_dev, cols_dev = features.shape
    vars_out = kernel.shape[0]
    n_row = lax.axis_size("row")
    n_col = lax.axis_size("col")
    len_x = rows_dev * n_row
    len_y = cols_dev * n_col
    f32 = jnp.float32
    bf16 = jnp.bfloat16
    offsets = [(first, second) for first in range(3) for second in range(3)]
    padded = extended(features, (("row", 2), ("col", 3)), 1)
    pred = jnp.zeros((samples, vars_out, rows_dev, cols_dev), f32)
    for first, second in offsets:
        window = padded[:, :, first : first + rows_dev, second : second + cols_dev]
        pred = pred + jnp.einsum(
            "vc,scxy->svxy", kernel[:, :, first, second], window, preferred_element_type=f32
        )
    pred_half = pred.astype(bf16)
    cos_y, sin_y = dft_tables(len_y)
    cos_x, sin_x = dft_tables(len_x)
    lines = lax.all_to_all(pred_half, "col", split_axis=2, concat_axis=3, tiled=True)
    half_re = jnp.einsum("svxy,ky->svxk", lines, cos_y, preferred_element_type=f32).astype(bf16)
    half_im = (-jnp.einsum("svxy,ky->svxk", lines, sin_y, preferred_element_type=f32)).astype(bf16)
    stacked = jnp.stack([half_re, half_im], axis=1)
    pencil = lax.all_to_all(stacked, ("row", "col"), split_axis=4, concat_axis=3, tiled=True)
    part_re = pencil[:, 0]
    part_im = pencil[:, 1]
    spec_re = jnp.einsum("kx,svxy->svyk", cos_x, part_re, preferred_element_type=f32) + jnp.einsum(
        "kx,svxy->svyk", sin_x, part_im, preferred_element_type=f32
    )
    spec_im = jnp.einsum("kx,svxy->svyk", cos_x, part_im, preferred_element_type=f32) - jnp.einsum(
        "kx,svxy->svyk", sin_x, part_re, preferred_element_type=f32
    )
    amp = jnp.sqrt(spec_re * spec_re + spec_im * spec_im + 1.0)
    factor = 2.0 * spec_weight[None] * (amp - target_amp) / amp
    grad_re = (factor * spec_re).astype(bf16)
    grad_im = (factor * spec_im).astype(bf16)
    back_re = (
        jnp.einsum("kx,svyk->svxy", cos_x, grad_re, preferred_element_type=f32)
        - jnp.einsum("kx,svyk->svxy", sin_x, grad_im, preferred_element_type=f32)
    ).astype(bf16)
    back_im = (
        jnp.einsum("kx,svyk->svxy", sin_x, grad_re, preferred_element_type=f32)
        + jnp.einsum("kx,svyk->svxy", cos_x, grad_im, preferred_element_type=f32)
    ).astype(bf16)
    backward = jnp.stack([back_re, back_im], axis=1)
    lines_back = lax.all_to_all(backward, ("row", "col"), split_axis=3, concat_axis=4, tiled=True)
    dpred_lines = jnp.einsum(
        "svxk,ky->svxy", lines_back[:, 0], cos_y, preferred_element_type=f32
    ) - jnp.einsum("svxk,ky->svxy", lines_back[:, 1], sin_y, preferred_element_type=f32)
    dpred_half = lax.all_to_all(
        dpred_lines.astype(bf16), "col", split_axis=3, concat_axis=2, tiled=True
    )
    kernel_terms = []
    for first, second in offsets:
        window = padded[:, :, first : first + rows_dev, second : second + cols_dev]
        kernel_terms.append(
            jnp.einsum("svxy,scxy->vc", dpred_half, window, preferred_element_type=f32)
        )
    kernel_local = jnp.stack(kernel_terms, axis=-1).reshape(vars_out, chans, 3, 3)
    summed = lax.psum(kernel_local, ("dp", "row", "col"))
    cells = lax.axis_size("dp") * samples * len_x * len_y
    kernel_grad = summed / cells
    padded_grad = extended(dpred_half, (("row", 2), ("col", 3)), 1)
    feature_full = jnp.zeros((samples, chans, rows_dev, cols_dev), f32)
    for first, second in offsets:
        window = padded_grad[
            :, :, 2 - first : 2 - first + rows_dev, 2 - second : 2 - second + cols_dev
        ]
        feature_full = feature_full + jnp.einsum(
            "vc,svxy->scxy", kernel[:, :, first, second], window, preferred_element_type=f32
        )
    return (kernel_grad, feature_full.astype(bf16))


def solution(mesh):
    return jax.shard_map(
        per_device,
        mesh=mesh,
        in_specs=(
            P("dp", None, "row", "col"),
            P(),
            P("dp", None, ("row", "col"), None),
            P(None, ("row", "col"), None),
        ),
        out_specs=(P(), P("dp", None, "row", "col")),
        check_vma=False,
    )
```

profile of v0, /device:TPU:1, one launch (start us, length us, event | category | flops | bytes accessed | tf_op | source)
XLA Modules:
  0.0 557.0 jit_solution(8465639277861265195)
XLA Ops:
  50.7 6.8 %fusion.109 = f32[192,128,8]{1,2,0:T(8,128)S(1)} fusion(bf16[1,96,194,1]{3,1,2,0:T(8,128)(2,1)} %copy.39, bf16[1,96,194,128]{3,1,2,0:T(8,128)(2,1)} %copy-done, bf16[8,96,3,3]{1,0,3,2:T(8,128)(2,1)S(1)} %copy-done.8), kind=kOutput, calls=%fused_computation.110 | convolution fusion | flops 47185920 | bytes 5593472 | tf_op jit(solution)/shard_map/vc,scxy->svxy/dot_general | solution.py:51
  68.3 10.3 %fusion.8 = (bf16[96,192,128]{2,0,1:T(8,128)(2,1)}, bf16[96,192,128]{2,0,1:T(8,128)(2,1)S(1)}, bf16[96,192,128]{2,0,1:T(8,128)(2,1)S(1)}) fusion(bf16[1,96,194,1]{3,1,2,0:T(8,128)(2,1)} %copy.36, bf16[1,96,194,128]{3,1,2,0:T(8,128)(2,1)S(1)} %bitcast.298, bf16[1,96,194,1]{3,1,2,0:T(8,128)(2,1)S(1)} %copy-done.1), kind=kLoop, calls=%fused_computation.20 | loop fusion | flops 28311552 | bytes 18998016 | tf_op jit(solution)/shard_map/reshape
  89.8 17.2 %all_to_all.69 = bf16[1,8,192,128]{3,1,0,2:T(8,128)(2,1)S(1)} all-to-all(bf16[1,8,192,128]{3,1,0,2:T(8,128)(2,1)S(1)} %fusion.67), channel_id=1, replica_groups=mesh['dp'=4,'row'=4,'col'=8] {'col'}, dimensions={2} | all-to-all | bytes 786432 | tf_op jit(solution)/shard_map/all_to_all | solution.py:57
  107.4 16.5 %fusion.76 = bf16[1,1,8,24,1024]{4,3,2,1,0:T(8,128)(2,1)S(1)} fusion(bf16[8,24,1024]{2,1,0:T(8,128)(2,1)S(1)} %reshape.187), kind=kOutput, calls=%fused_computation.82 | convolution fusion | flops 419823616 | bytes 786432 | tf_op jit(solution)/shard_map/svxy,ky->svxk/dot_general | solution.py:59
  123.9 16.3 %fusion.73 = bf16[1,1,8,24,1024]{4,3,2,1,0:T(8,128)(2,1)S(1)} fusion(bf16[8,24,1024]{2,1,0:T(8,128)(2,1)S(1)} %reshape.187), kind=kOutput, calls=%fused_computation.81 | convolution fusion | flops 419627008 | bytes 786432 | tf_op jit(solution)/shard_map/svxy,ky->svxk/dot_general | solution.py:58
  145.0 7.4 %reshape.238 = bf16[32,2,6144]{2,1,0:T(2,128)(2,1)S(1)} reshape(bf16[1024,1,2,8,24]{4,3,2,1,0:T(8,128)(2,1)} %bitcast.329) | data formatting | bytes 1572864
  152.4 19.1 %all_to_all.70 = bf16[32,2,6144]{2,1,0:T(2,128)(2,1)S(1)} all-to-all(bf16[32,2,6144]{2,1,0:T(2,128)(2,1)S(1)} %reshape.238), channel_id=1, replica_groups=mesh['dp'=4,'row'=4,'col'=8] {'row','col'}, dimensions={0} | all-to-all | bytes 1572864 | tf_op jit(solution)/shard_map/all_to_all | solution.py:61
  171.5 7.0 %reshape.239 = bf16[1024,1,2,8,24]{4,3,2,1,0:T(8,128)(2,1)} reshape(bf16[32,2,6144]{2,1,0:T(2,128)(2,1)S(1)} %all_to_all.70) | data formatting | bytes 1572864
  178.4 6.9 %copy.63 = bf16[1,2,8,24,32,32]{3,4,5,2,1,0:T(8,128)(2,1)} copy(bf16[1,2,8,24,32,32]{3,2,1,5,4,0:T(8,128)(2,1)} %bitcast.330) | data formatting | bytes 1572864 | tf_op jit(solution)/shard_map/all_to_all | solution.py:61
  192.2 9.2 %fusion.89 = f32[8,32,768]{2,1,0:T(8,128)S(1)} fusion(bf16[1,2,8,768,32]{3,4,2,1,0:T(8,128)(2,1)S(1)} %all_to_all.56), kind=kOutput, calls=%fused_computation.87 | convolution fusion | flops 308477952 | bytes 1179648 | tf_op jit(solution)/shard_map/kx,svxy->svyk/dot_general | solution.py:67
  201.4 9.4 %fusion.91 = f32[8,32,768]{2,1,0:T(8,128)S(1)} fusion(bf16[1,2,8,768,32]{3,4,2,1,0:T(8,128)(2,1)S(1)} %all_to_all.56), kind=kOutput, calls=%fused_computation.88 | convolution fusion | flops 308477952 | bytes 1179648 | tf_op jit(solution)/shard_map/kx,svxy->svyk/dot_general | solution.py:64
  210.8 9.8 %convolution_subtract_fusion.1 = f32[8,32,768]{2,1,0:T(8,128)S(1)} fusion(f32[8,32,768]{2,1,0:T(8,128)S(1)} %fusion.89, bf16[1,2,8,768,32]{3,4,2,1,0:T(8,128)(2,1)S(1)} %all_to_all.56), kind=kOutput, calls=%fused_computation.67 | convolution fusion | flops 308674560 | bytes 1966080 | tf_op jit(solution)/shard_map/kx,svxy->svyk/dot_general | solution.py:67
  220.6 9.8 %fusion.112 = (bf16[8,32,768]{2,1,0:T(8,128)(2,1)S(1)}, bf16[8,32,768]{2,1,0:T(8,128)(2,1)S(1)}) fusion(f32[8,32,768]{2,1,0:T(8,128)S(1)} %convolution_subtract_fusion.1, f32[1,8,32,768]{3,2,1,0:T(8,128)S(1)} %copy-done.9, f32[8,32,768]{2,1,0:T(8,128)S(1)} %copy-done.10, f32[8,32,768]{2,1,0:T(8,128)S(1)} %fusion.91, ...), kind=kOutput, calls=%fused_computation.113 | convolution fusion | flops 311033856 | bytes 4325376 | tf_op jit(solution)/shard_map/kx,svxy->svyk/dot_general | solution.py:64
  230.4 9.9 %fusion.81 = f32[8,32,768]{2,1,0:T(8,128)S(1)} fusion(bf16[8,32,768]{2,1,0:T(8,128)(2,1)S(1)} %get-tuple-element.16), kind=kOutput, calls=%fused_computation.85 | convolution fusion | flops 308477952 | bytes 1179648 | tf_op jit(solution)/shard_map/kx,svyk->svxy/dot_general | solution.py:79
  240.3 9.6 %fusion.87 = f32[8,32,768]{2,1,0:T(8,128)S(1)} fusion(bf16[8,32,768]{2,1,0:T(8,128)(2,1)S(1)} %get-tuple-element.16), kind=kOutput, calls=%fused_computation.86 | convolution fusion | flops 308477952 | bytes 1179648 | tf_op jit(solution)/shard_map/kx,svyk->svxy/dot_general | solution.py:75
  249.9 10.2 %fusion.68 = bf16[1,1,8,768,32]{3,4,2,1,0:T(8,128)(2,1)S(1)} fusion(f32[8,32,768]{2,1,0:T(8,128)S(1)} %fusion.81, bf16[8,32,768]{2,1,0:T(8,128)(2,1)S(1)} %get-tuple-element.15), kind=kOutput, calls=%fused_computation.78 | convolution fusion | flops 308871168 | bytes 1572864 | tf_op jit(solution)/shard_map/kx,svyk->svxy/dot_general | solution.py:80
  260.2 10.3 %fusion.69 = bf16[1,1,8,768,32]{3,4,2,1,0:T(8,128)(2,1)S(1)} fusion(f32[8,32,768]{2,1,0:T(8,128)S(1)} %fusion.87, bf16[8,32,768]{2,1,0:T(8,128)(2,1)S(1)} %get-tuple-element.15), kind=kOutput, calls=%fused_computation.79 | convolution fusion | flops 308871168 | bytes 1572864 | tf_op jit(solution)/shard_map/kx,svyk->svxy/dot_general | solution.py:76
  279.0 19.1 %all_to_all.71 = bf16[32,2,6144]{2,1,0:T(2,128)(2,1)} all-to-all(bf16[32,2,6144]{2,1,0:T(2,128)(2,1)} %reshape.240), channel_id=1, replica_groups=mesh['dp'=4,'row'=4,'col'=8] {'row','col'}, dimensions={0} | all-to-all | bytes 1572864 | tf_op jit(solution)/shard_map/all_to_all | solution.py:83
  307.9 10.1 %copy.48 = bf16[1,2,8,24,32,32]{5,4,3,2,1,0:T(8,128)(2,1)S(1)} copy(bf16[1,2,8,24,32,32]{3,4,5,2,1,0:T(8,128)(2,1)} %bitcast.328) | data formatting | bytes 1572864 | tf_op jit(solution)/shard_map/all_to_all | solution.py:83
  322.4 17.0 %fusion.38 = f32[8,24,1024]{2,1,0:T(8,128)S(1)} fusion(bf16[1,2,8,24,1024]{4,3,2,1,0:T(8,128)(2,1)} %all_to_all.60), kind=kOutput, calls=%fused_computation.57 | convolution fusion | flops 419430400 | bytes 1179648 | tf_op jit(solution)/shard_map/svxk,ky->svxy/dot_general | solution.py:86
  339.4 15.7 %fusion.70 = bf16[1,8,24,1024]{3,2,1,0:T(8,128)(2,1)S(1)} fusion(f32[8,24,1024]{2,1,0:T(8,128)S(1)} %fusion.38, bf16[1,2,8,24,1024]{4,3,2,1,0:T(8,128)(2,1)S(1)} %copy-done.7), kind=kOutput, calls=%fused_computation.80 | convolution fusion | flops 419823616 | bytes 1572864 | tf_op jit(solution)/shard_map/svxk,ky->svxy/dot_general | solution.py:84
  359.6 11.2 %all_to_all.72 = bf16[8,2,12288]{2,1,0:T(2,128)(2,1)S(1)} all-to-all(bf16[8,2,12288]{2,1,0:T(2,128)(2,1)S(1)} %reshape.242), channel_id=1, replica_groups=mesh['dp'=4,'row'=4,'col'=8] {'col'}, dimensions={0} | all-to-all | bytes 786432 | tf_op jit(solution)/shard_map/all_to_all | solution.py:87
  404.7 65.7 %psum.7 = f32[8,96,3,3]{1,0,3,2:T(8,128)S(1)} all-reduce(f32[8,96,3,3]{1,0,3,2:T(8,128)S(1)} %bitcast.342), channel_id=1, replica_groups=mesh['dp'=4,'row'=4,'col'=8] {'dp','row','col'}, use_global_device_ids=true, to_apply=%region_0.1 | all-reduce | flops 6912 | bytes 55296 | tf_op jit(solution)/shard_map/psum | solution.py:97
  523.5 26.9 %fusion = bf16[1,96,192,128]{3,1,2,0:T(8,128)(2,1)} fusion(f32[192,128,96]{1,2,0:T(8,128)} %fusion.115, f32[192,128,96]{1,2,0:T(8,128)} %fusion.118, f32[192,128,96]{1,2,0:T(8,128)} %fusion.119, f32[192,128,96]{1,2,0:T(8,128)} %fusion.135, f32[192,128,96]{1,2,0:T(8,128)} %fusion.120, f32[192,128,96]{1,2,0:T(8,128)} %fusion.121, ...), kind=kOutput, calls=%fused_computation.12 | convolution fusion | flops 58982400 | bytes 80611328 | tf_op jit(solution)/shard_map/vc,svxy->scxy/dot_general | solution.py:106
  (139 shorter events, 204.3 us)
Async XLA Ops:
  0.6 12.6 %copy-start.2 = (bf16[1,96,192,128]{3,2,1,0:T(8,128)(2,1)S(1)}, bf16[1,96,192,128]{3,2,1,0:T(8,128)(2,1)}, u32[]{:S(2)}) copy-start(bf16[1,96,192,128]{3,2,1,0:T(8,128)(2,1)} %param.4) | copy-start | bytes 14155780
  0.6 12.6 %copy-start.8 = (bf16[8,96,3,3]{1,0,3,2:T(8,128)(2,1)S(1)}, bf16[8,96,3,3]{1,0,3,2:T(8,128)(2,1)}, u32[]{:S(2)}) copy-start(bf16[8,96,3,3]{1,0,3,2:T(8,128)(2,1)} %param.5) | copy-start | bytes 41476
  6.2 13.0 %copy-start.5 = (bf16[1,96,192,128]{3,1,2,0:T(8,128)(2,1)}, bf16[1,96,192,128]{3,1,2,0:T(8,128)(2,1)S(1)}, u32[]{:S(2)}) copy-start(bf16[1,96,192,128]{3,1,2,0:T(8,128)(2,1)S(1)} %copy.32) | copy-start | bytes 14155780
  6.2 13.0 %collective-permute-start.1 = (bf16[1,96,1,128]{3,1,2,0:T(8,128)(2,1)S(1)}, bf16[1,96,1,128]{3,1,2,0:T(8,128)(2,1)S(1)}, u32[]{:S(2)}, u32[]{:S(2)}) collective-permute-start(bf16[1,96,1,128]{3,1,2,0:T(8,128)(2,1)S(1)} %get-tuple-element.13), channel_id=1, source_target_pairs={{8,0},{16,8},{24,16},{9,1},{17,9},{25,17},{10,2},{18,10},{26,18},{... | collective-permute-start | bytes 73736 | tf_op jit(solution)/shard_map/ppermute | solution.py:19
  9.5 6.3 %collective-permute-start = (bf16[1,96,1,128]{3,1,2,0:T(8,128)(2,1)S(1)}, bf16[1,96,1,128]{3,1,2,0:T(8,128)(2,1)S(1)}, u32[]{:S(2)}, u32[]{:S(2)}) collective-permute-start(bf16[1,96,1,128]{3,1,2,0:T(8,128)(2,1)S(1)} %get-tuple-element.14), channel_id=1, source_target_pairs={{0,8},{8,16},{16,24},{1,9},{9,17},{17,25},{2,10},{10,18},{18,26},{... | collective-permute-start | bytes 73736 | tf_op jit(solution)/shard_map/ppermute | solution.py:17
  29.5 15.0 %slice-start.14 = ((s8[4718592]{0:T(1024)(128)(4,1)}), s8[524288]{0:T(1024)(128)(4,1)S(1)}, s32[]{:S(2)}) async-start(s8[4718592]{0:T(1024)(128)(4,1)} %bitcast.336), calls=%async_computation.18 | async-start | bytes 1048576
  34.3 10.2 %slice-start.15 = ((s8[4718592]{0:T(1024)(128)(4,1)}), s8[4194304]{0:T(1024)(128)(4,1)S(1)}, s32[]{:S(2)}) async-start(s8[4718592]{0:T(1024)(128)(4,1)} %bitcast.336), calls=%async_computation.19 | async-start | bytes 8388608
  34.3 11.8 %collective-permute-start.3 = (bf16[1,96,194,1]{2,1,3,0:T(8,128)(2,1)S(1)}, bf16[1,96,194,1]{2,1,3,0:T(8,128)(2,1)S(1)}, u32[]{:S(2)}, u32[]{:S(2)}) collective-permute-start(bf16[1,96,194,1]{2,1,3,0:T(8,128)(2,1)S(1)} %copy.38), channel_id=1, source_target_pairs={{1,0},{2,1},{3,2},{4,3},{5,4},{6,5},{7,6},{9,8},{10,9},{11,10},{12... | collective-permute-start | bytes 111752 | tf_op jit(solution)/shard_map/ppermute | solution.py:19
  35.9 21.6 %collective-permute-start.2 = (bf16[1,96,194,1]{2,1,3,0:T(8,128)(2,1)S(1)}, bf16[1,96,194,1]{2,1,3,0:T(8,128)(2,1)S(1)}, u32[]{:S(2)}, u32[]{:S(2)}) collective-permute-start(bf16[1,96,194,1]{2,1,3,0:T(8,128)(2,1)S(1)} %copy.35), channel_id=1, source_target_pairs={{0,1},{1,2},{2,3},{3,4},{4,5},{5,6},{6,7},{8,9},{9,10},{10,11},{11... | collective-permute-start | bytes 111752 | tf_op jit(solution)/shard_map/ppermute | solution.py:17
  57.5 10.5 %slice-start = ((s8[4767744]{0:T(1024)(128)(4,1)}), s8[573440]{0:T(1024)(128)(4,1)S(1)}, s32[]{:S(2)}) async-start(s8[4767744]{0:T(1024)(128)(4,1)} %bitcast.297), calls=%async_computation.4 | async-start | bytes 1146880
  78.6 7.1 %copy-start.3 = (bf16[96,192,128]{2,0,1:T(8,128)(2,1)}, bf16[96,192,128]{2,0,1:T(8,128)(2,1)S(1)}, u32[]{:S(2)}) copy-start(bf16[96,192,128]{2,0,1:T(8,128)(2,1)S(1)} %get-tuple-element.9) | copy-start | bytes 14155780
  78.6 7.1 %copy-start.4 = (bf16[96,192,128]{2,0,1:T(8,128)(2,1)}, bf16[96,192,128]{2,0,1:T(8,128)(2,1)S(1)}, u32[]{:S(2)}) copy-start(bf16[96,192,128]{2,0,1:T(8,128)(2,1)S(1)} %get-tuple-element.10) | copy-start | bytes 14155780
  210.8 9.8 %copy-start.9 = (f32[1,8,32,768]{3,2,1,0:T(8,128)S(1)}, f32[1,8,32,768]{3,2,1,0:T(8,128)}, u32[]{:S(2)}) copy-start(f32[1,8,32,768]{3,2,1,0:T(8,128)} %param.6) | copy-start | bytes 2359300
  210.8 9.8 %copy-start.10 = (f32[8,32,768]{2,1,0:T(8,128)S(1)}, f32[8,32,768]{2,1,0:T(8,128)}, u32[]{:S(2)}) copy-start(f32[8,32,768]{2,1,0:T(8,128)} %param.7) | copy-start | bytes 2359300
  322.4 17.0 %copy-start.7 = (bf16[1,2,8,24,1024]{4,3,2,1,0:T(8,128)(2,1)S(1)}, bf16[1,2,8,24,1024]{4,3,2,1,0:T(8,128)(2,1)}, u32[]{:S(2)}) copy-start(bf16[1,2,8,24,1024]{4,3,2,1,0:T(8,128)(2,1)} %all_to_all.60) | copy-start | bytes 2359300
  375.4 13.5 %slice-start.12 = ((s8[4718592]{0:T(1024)(128)(4,1)}), s8[4194304]{0:T(1024)(128)(4,1)S(1)}, s32[]{:S(2)}) async-start(s8[4718592]{0:T(1024)(128)(4,1)} %bitcast.326), calls=%async_computation.16 | async-start | bytes 8388608
  379.2 9.7 %slice-start.13 = ((s8[4718592]{0:T(1024)(128)(4,1)}), s8[524288]{0:T(1024)(128)(4,1)S(1)}, s32[]{:S(2)}) async-start(s8[4718592]{0:T(1024)(128)(4,1)} %bitcast.326), calls=%async_computation.17 | async-start | bytes 1048576
  379.2 11.1 %slice-start.10 = ((s8[4718592]{0:T(1024)(128)(4,1)}), s8[4194304]{0:T(1024)(128)(4,1)S(1)}, s32[]{:S(2)}) async-start(s8[4718592]{0:T(1024)(128)(4,1)} %bitcast.324), calls=%async_computation.14 | async-start | bytes 8388608
  379.2 12.4 %slice-start.8 = ((s8[4718592]{0:T(1024)(128)(4,1)}), s8[4194304]{0:T(1024)(128)(4,1)S(1)}, s32[]{:S(2)}) async-start(s8[4718592]{0:T(1024)(128)(4,1)} %bitcast.321), calls=%async_computation.12 | async-start | bytes 8388608
  391.7 8.4 %slice-start.16 = ((s8[4718592]{0:T(1024)(128)(4,1)}), s8[4194304]{0:T(1024)(128)(4,1)S(1)}, s32[]{:S(2)}) async-start(s8[4718592]{0:T(1024)(128)(4,1)} %bitcast.338), calls=%async_computation.20 | async-start | bytes 8388608
  470.4 6.2 %collective-permute-start.5 = (bf16[1,8,1,128]{3,1,2,0:T(8,128)(2,1)S(1)}, bf16[1,8,1,128]{3,1,2,0:T(8,128)(2,1)S(1)}, u32[]{:S(2)}, u32[]{:S(2)}) collective-permute-start(bf16[1,8,1,128]{3,1,2,0:T(8,128)(2,1)S(1)} %get-tuple-element.21), channel_id=1, source_target_pairs={{8,0},{16,8},{24,16},{9,1},{17,9},{25,17},{10,2},{18,10},{26,18},{... | collective-permute-start | bytes 6152 | tf_op jit(solution)/shard_map/ppermute | solution.py:19
  473.0 3.7 collective-permute-start.4
  476.9 20.9 %collective-permute-start.7 = (bf16[1,8,194,1]{3,1,2,0:T(8,128)(2,1)S(1)}, bf16[1,8,194,1]{3,1,2,0:T(8,128)(2,1)S(1)}, u32[]{:S(2)}, u32[]{:S(2)}) collective-permute-start(bf16[1,8,194,1]{3,1,2,0:T(8,128)(2,1)S(1)} %get-tuple-element.19), channel_id=1, source_target_pairs={{0,1},{1,2},{2,3},{3,4},{4,5},{5,6},{6,7},{8,9},{9,10},{10,11},{11... | collective-permute-start | bytes 9320 | tf_op jit(solution)/shard_map/ppermute | solution.py:17
  481.2 16.7 %collective-permute-start.6 = (bf16[1,8,194,1]{3,1,2,0:T(8,128)(2,1)S(1)}, bf16[1,8,194,1]{3,1,2,0:T(8,128)(2,1)S(1)}, u32[]{:S(2)}, u32[]{:S(2)}) collective-permute-start(bf16[1,8,194,1]{3,1,2,0:T(8,128)(2,1)S(1)} %get-tuple-element.20), channel_id=1, source_target_pairs={{1,0},{2,1},{3,2},{4,3},{5,4},{6,5},{7,6},{9,8},{10,9},{11,10},{12... | collective-permute-start | bytes 9320 | tf_op jit(solution)/shard_map/ppermute | solution.py:19
  (13 other events, 64.8 us)
where the time goes:
time: 563 us; the launch traced here: 557 us
  matrix products  266 us (47%)
  blocking collectives  132 us (23%)
  local copies, waits for them, and re-layouts  114 us (20%)
  starting transfers between devices  25.1 us (4%)
  other arithmetic  12.5 us (2%)
    dot_general x9, matrix products, per_device(): jnp.einsum('vc,svxy->scxy', kernel[:, :, first, second], window, preferre...  68.2 us
    psum x1, blocking collectives, per_device(): summed = lax.psum(kernel_local, ('dp', 'row', 'col'))  65.7 us
    unnamed x68, local copies, waits for them, and re-layouts  43.4 us
    dot_general x9, matrix products, per_device(): jnp.einsum('vc,scxy->svxy', kernel[:, :, first, second], window, preferre...  31.5 us
    dot_general x9, matrix products, per_device(): jnp.einsum('svxy,scxy->vc', dpred_half, window, preferred_element_type=f32)  23 us
    all_to_all x3, local copies, waits for them, and re-layouts, per_device(): lax.all_to_all(backward, ('row', 'col'), split_axis=3, concat_axis=4, til...  20.3 us
    all_to_all x1, blocking collectives, per_device(): lax.all_to_all(stacked, ('row', 'col'), split_axis=4, concat_axis=3, tile...  19.1 us
    all_to_all x1, blocking collectives, per_device(): lax.all_to_all(backward, ('row', 'col'), split_axis=3, concat_axis=4, til...  19.1 us
  transfers between devices with their start and end apart: 8, of which 2 were waited for; matrix products, arithmetic and copies ran while one was open for 6% of the time, Pallas kernels for 0%

commit v1 on v0

v1 whole, which is shorter than its diff:
```python
import math

import jax
import jax.numpy as jnp
import ml_dtypes
import numpy as np
from jax import lax
from jax.experimental import pallas as pl
from jax.experimental.pallas import tpu as pltpu
from jax.sharding import PartitionSpec as P

MESH = pl.DeviceIdType.MESH
F32 = jnp.float32
BF16 = jnp.bfloat16
VMEM_LIMIT = 56 * 1024 * 1024

C = 96
V = 8
NX = 768
NY = 1024
NDP = 4
NROW = 4
NCOL = 8
XB = NX // NROW
YB = NY // NCOL
QB = NY // (NROW * NCOL)
GROUP = 16
GROUPS = XB // GROUP
PACK = 2 * XB


def dft_tables(length):
    index = np.arange(length, dtype=np.int64)
    product = (index[:, None] * index[None, :]) % length
    angles = product * (2.0 * math.pi / length)
    factor = 1.0 / math.sqrt(length)
    return np.cos(angles) * factor, np.sin(angles) * factor


def spectral_tables():
    cos_y, sin_y = dft_tables(NY)
    along_y = np.concatenate([cos_y, -sin_y], axis=0)
    rim = np.zeros((2 * NY, 16 * NCOL))
    for k in range(NCOL):
        if k > 0:
            rim[:, 16 * k] = along_y[:, YB * k - 1]
        if k < NCOL - 1:
            rim[:, 16 * k + 1] = along_y[:, YB * (k + 1)]
    cos_x, sin_x = dft_tables(NX)
    from_re = np.concatenate([cos_x, -sin_x], axis=0).T.reshape(NX // 64, 64, 2 * NX)
    from_im = np.concatenate([sin_x, cos_x], axis=0).T.reshape(NX // 64, 64, 2 * NX)
    along_x = np.stack([from_re, from_im], axis=1).reshape(2 * NX, 2 * NX)
    bf16 = ml_dtypes.bfloat16
    return along_y.astype(bf16), rim.astype(bf16), along_x.astype(bf16)


def mm(a, b):
    return lax.dot_general(a, b, (((1,), (0,)), ((), ())), preferred_element_type=F32)


def mm_nt(a, b):
    return lax.dot_general(a, b, (((1,), (1,)), ((), ())), preferred_element_type=F32)


def lanes(shape):
    return lax.broadcasted_iota(jnp.int32, shape, len(shape) - 1)


def pick(row_lane_pairs, rows=16, width=128):
    r = lax.broadcasted_iota(jnp.int32, (rows, width), 0)
    c = lax.broadcasted_iota(jnp.int32, (rows, width), 1)
    hit = jnp.zeros((rows, width), F32)
    for row, lane in row_lane_pairs:
        hit = jnp.where((r == row) & (c == lane), 1.0, hit)
    return hit.astype(BF16)


def conv_kernel(feat, w, ft, pred, halo, turn, taps, whole, rim, send, recv):
    step = pl.program_id(0)
    row = lax.axis_index("row")
    up = lax.rem(row + NROW - 1, NROW)
    down = lax.rem(row + 1, NROW)
    group = jnp.where(step == 0, 0, jnp.where(step == 1, GROUPS - 1, step - 1))

    to_down = pltpu.make_async_remote_copy(
        src_ref=taps.at[XB, 0:24], dst_ref=taps.at[0, 0:24],
        send_sem=send.at[0], recv_sem=recv.at[0], device_id={"row": down}, device_id_type=MESH)
    to_up = pltpu.make_async_remote_copy(
        src_ref=taps.at[1, 48:72], dst_ref=taps.at[XB + 1, 48:72],
        send_sem=send.at[1], recv_sem=recv.at[1], device_id={"row": up}, device_id_type=MESH)

    @pl.when(step == 0)
    def _():
        barrier = pltpu.get_barrier_semaphore()
        pl.semaphore_signal(barrier, inc=1, device_id={"row": up}, device_id_type=MESH)
        pl.semaphore_signal(barrier, inc=1, device_id={"row": down}, device_id_type=MESH)
        pl.semaphore_wait(barrier, 2)

    turn[...] = feat[...].astype(F32).reshape(C * GROUP, YB)
    for x in range(GROUP):
        ft[x] = turn[pl.ds(x, C, stride=GROUP), :].astype(BF16)
    for pair in range(GROUP // 2):
        both = jnp.concatenate([ft[2 * pair], ft[2 * pair + 1]], axis=1)
        got = mm(w[...], both)
        taps[1 + GROUP * group + 2 * pair] = got[0:72, 0:YB]
        taps[2 + GROUP * group + 2 * pair] = got[0:72, YB : 2 * YB]

    @pl.when(step == 1)
    def _():
        to_down.start()
        to_up.start()

    @pl.when(step == GROUPS - 1)
    def _():
        to_down.wait()
        to_up.wait()

        @pl.when(row == 0)
        def _():
            taps[0, 0:24] = jnp.zeros((24, YB), F32)

        @pl.when(row == NROW - 1)
        def _():
            taps[XB + 1, 48:72] = jnp.zeros((24, YB), F32)

        lane = lanes((V * GROUP, YB))

        def combine(g, carry):
            x = GROUP * g
            total = (taps[pl.ds(x, GROUP), 0:24] + taps[pl.ds(x + 1, GROUP), 24:48]
                     + taps[pl.ds(x + 2, GROUP), 48:72])
            left = total[:, 0:8].reshape(V * GROUP, YB)
            mid = total[:, 8:16].reshape(V * GROUP, YB)
            right = total[:, 16:24].reshape(V * GROUP, YB)
            left = pltpu.roll(left, 1, 1)
            right = pltpu.roll(right, YB - 1, 1)
            at = pl.ds(pl.multiple_of(V * GROUP * g, V * GROUP), V * GROUP)
            whole[at, :] = mid + jnp.where(lane == 0, 0.0, left) + jnp.where(lane == YB - 1, 0.0, right)
            rim[at, :] = jnp.where(lane == 0, left, right)
            return carry

        lax.fori_loop(0, GROUPS, combine, 0)
        chosen = pick([(0, YB - 1), (1, 0)])
        for v in range(V):
            pred[v] = whole[pl.ds(v, XB, stride=V), :].astype(BF16)
            edge = mm_nt(chosen, rim[pl.ds(v, XB, stride=V), :].astype(BF16))
            halo[v] = jnp.concatenate([edge, jnp.zeros((16, 256 - XB), F32)], axis=1).astype(BF16)


def convolve(features, weights):
    def place(i):
        return jnp.where(i == 0, 0, jnp.where(i == 1, GROUPS - 1, i - 1))

    return pl.pallas_call(
        conv_kernel,
        grid=(GROUPS,),
        in_specs=[
            pl.BlockSpec((C, GROUP, YB), lambda i: (0, place(i), 0)),
            pl.BlockSpec((80, C), lambda i: (0, 0)),
        ],
        out_specs=[
            pl.BlockSpec((GROUP, C, YB), lambda i: (place(i), 0, 0)),
            pl.BlockSpec((V, XB, YB), lambda i: (0, 0, 0)),
            pl.BlockSpec((V, 16, 256), lambda i: (0, 0, 0)),
        ],
        out_shape=[
            jax.ShapeDtypeStruct((XB, C, YB), BF16),
            jax.ShapeDtypeStruct((V, XB, YB), BF16),
            jax.ShapeDtypeStruct((V, 16, 256), BF16),
        ],
        scratch_shapes=[
            pltpu.VMEM((C * GROUP, YB), F32),
            pltpu.VMEM((XB + 2, 72, YB), F32),
            pltpu.VMEM((XB * V, YB), F32),
            pltpu.VMEM((XB * V, YB), F32),
            pltpu.SemaphoreType.DMA((2,)),
            pltpu.SemaphoreType.DMA((2,)),
        ],
        compiler_params=pltpu.CompilerParams(
            collective_id=0, has_side_effects=True, vmem_limit_bytes=VMEM_LIMIT),
        name="convolve",
    )(features, weights)


def spectral_kernel(pred, halo, t1_hbm, rim_hbm, t2_hbm, targ_hbm, wt_hbm, tiles, rims,
                    t1, t1rim, t2, targ, wt, lines, rim_in, half, spec, grads, back, coef, flat,
                    dp_out, rim_out,
                    load, s1, r1, s1h, r1h, s2, r2, s3, r3, s4, r4, s4h, r4h):
    row = lax.axis_index("row")
    col = lax.axis_index("col")
    me = NCOL * row + col
    everyone = NROW * NCOL

    loads = [pltpu.make_async_copy(src, dst, load.at[n]) for n, (src, dst) in enumerate(
        [(t1_hbm, t1), (rim_hbm, t1rim), (t2_hbm, t2), (targ_hbm, targ), (wt_hbm, wt)])]
    for one in loads:
        one.start()

    barrier = pltpu.get_barrier_semaphore()

    def greet(d, carry):
        other = lax.rem(me + d, everyone)
        pl.semaphore_signal(barrier, inc=1, device_id={"row": other // NCOL, "col": lax.rem(other, NCOL)},
                            device_id_type=MESH)
        return carry

    lax.fori_loop(1, everyone, greet, 0)
    pl.semaphore_wait(barrier, everyone - 1)

    def line_copy(k, source):
        return pltpu.make_async_remote_copy(
            src_ref=pred.at[k], dst_ref=lines.at[0:XB, pl.ds(pl.multiple_of(YB * source, YB), YB)],
            send_sem=s1.at[k], recv_sem=r1.at[source], device_id={"col": k}, device_id_type=MESH)

    def line_rim_copy(k, source):
        return pltpu.make_async_remote_copy(
            src_ref=halo.at[k], dst_ref=rim_in.at[pl.ds(pl.multiple_of(16 * source, 16), 16), :],
            send_sem=s1h.at[k], recv_sem=r1h.at[source], device_id={"col": k}, device_id_type=MESH)

    def send_lines(d, carry):
        k = lax.rem(col + d, NCOL)
        line_copy(k, col).start()
        line_rim_copy(k, col).start()
        return carry

    lax.fori_loop(1, NCOL, send_lines, 0)
    own_line = pltpu.make_async_copy(
        pred.at[col], lines.at[0:XB, pl.ds(pl.multiple_of(YB * col, YB), YB)], r1.at[col])
    own_rim = pltpu.make_async_copy(
        halo.at[col], rim_in.at[pl.ds(pl.multiple_of(16 * col, 16), 16), :], r1h.at[col])
    own_line.start()
    own_rim.start()
    lines[XB:256, :] = jnp.zeros((256 - XB, NY), BF16)
    loads[0].wait()
    loads[1].wait()
    own_line.wait()
    own_rim.wait()

    def wait_lines(d, carry):
        k = lax.rem(col + d, NCOL)
        line_copy(k, k).wait_recv()
        line_rim_copy(k, k).wait_recv()
        return carry

    lax.fori_loop(1, NCOL, wait_lines, 0)

    def half_copy(j, source):
        return pltpu.make_async_remote_copy(
            src_ref=half.at[pl.ds(pl.multiple_of(QB * j, QB), QB), :],
            dst_ref=spec.at[pl.ds(pl.multiple_of(QB * lax.rem(source, NCOL), QB), QB),
                            pl.ds(pl.multiple_of(PACK * (source // NCOL), PACK), PACK)],
            send_sem=s2.at[j], recv_sem=r2.at[source],
            device_id={"row": j // NCOL, "col": lax.rem(j, NCOL)}, device_id_type=MESH)

    own_half = pltpu.make_async_copy(
        half.at[pl.ds(pl.multiple_of(QB * me, QB), QB), :],
        spec.at[pl.ds(pl.multiple_of(QB * col, QB), QB), pl.ds(pl.multiple_of(PACK * row, PACK), PACK)],
        r2.at[me])
    first64 = lanes((128, 128)) < 64

    def along_y(c, carry):
        chunk = lax.rem(c + me // 4 + 1, 8)
        q = pl.multiple_of(128 * chunk, 128)
        re = mm_nt(t1[pl.ds(q, 128), :], lines[...]) + mm(t1rim[pl.ds(q, 128), :], rim_in[...])
        im = mm_nt(t1[pl.ds(NY + q, 128), :], lines[...]) + mm(t1rim[pl.ds(NY + q, 128), :], rim_in[...])
        re0, re1 = re[:, 0:128], re[:, 128:256]
        im0, im1 = im[:, 0:128], im[:, 128:256]
        half[pl.ds(q, 128), 0:128] = jnp.where(first64, re0, pltpu.roll(im0, 64, 1)).astype(BF16)
        half[pl.ds(q, 128), 128:256] = jnp.where(first64, pltpu.roll(re0, 64, 1), im0).astype(BF16)
        half[pl.ds(q, 128), 256:384] = jnp.where(first64, re1, pltpu.roll(im1, 64, 1)).astype(BF16)
        for m in range(4):
            j = 4 * chunk + m

            @pl.when(j != me)
            def _():
                half_copy(j, me).start()

            @pl.when(j == me)
            def _():
                own_half.start()

        return carry

    lax.fori_loop(0, 8, along_y, 0)
    loads[2].wait()
    loads[3].wait()
    loads[4].wait()
    own_half.wait()

    def wait_half(d, carry):
        other = lax.rem(me + d, everyone)
        half_copy(other, other).wait_recv()
        return carry

    lax.fori_loop(1, everyone, wait_half, 0)

    def along_x(c, carry):
        p = pl.ds(pl.multiple_of(256 * c, 256), 256)
        p_im = pl.ds(pl.multiple_of(NX + 256 * c, 256), 256)
        re = mm(spec[...], t2[:, p])
        im = mm(spec[...], t2[:, p_im])
        amp = jnp.sqrt(re * re + im * im + 1.0)
        factor = 2.0 * wt[:, p] * (amp - targ[:, p]) / amp
        grads[:, p] = (factor * re).astype(BF16)
        grads[:, p_im] = (factor * im).astype(BF16)
        return carry

    lax.fori_loop(0, 3, along_x, 0)

    def back_copy(r, v, source):
        return pltpu.make_async_remote_copy(
            src_ref=back.at[r, pl.ds(pl.multiple_of(QB * v, QB), QB), :],
            dst_ref=coef.at[pl.ds(pl.multiple_of(QB * source, QB), QB), :],
            send_sem=s3.at[NCOL * r + v], recv_sem=r3.at[source],
            device_id={"row": r, "col": v}, device_id_type=MESH)

    own_back = pltpu.make_async_copy(
        back.at[row, pl.ds(pl.multiple_of(QB * col, QB), QB), :],
        coef.at[pl.ds(pl.multiple_of(QB * me, QB), QB), :], r3.at[me])

    def back_x(c, carry):
        r = lax.rem(row + 1 + c, NROW)
        back[r] = mm_nt(grads[...], t2[pl.ds(pl.multiple_of(PACK * r, PACK), PACK), :]).astype(BF16)
        for d in range(NCOL):
            v = lax.rem(col + d, NCOL)
            if d > 0:
                back_copy(r, v, me).start()
            else:
                @pl.when(r != row)
                def _():
                    back_copy(r, v, me).start()

                @pl.when(r == row)
                def _():
                    own_back.start()

        return carry

    lax.fori_loop(0, NROW, back_x, 0)
    own_back.wait()

    def wait_back(d, carry):
        other = lax.rem(me + d, everyone)
        back_copy(other // NCOL, lax.rem(other, NCOL), other).wait_recv()
        return carry

    lax.fori_loop(1, everyone, wait_back, 0)

    for b in range(3):
        turned = coef[:, 128 * b : 128 * b + 128].T
        flat[64 * b : 64 * b + 64, 0:NY] = turned[0:64]
        flat[64 * b : 64 * b + 64, NY : 2 * NY] = turned[64:128]

    def tile_copy(k, source):
        return pltpu.make_async_remote_copy(
            src_ref=dp_out.at[k], dst_ref=tiles.at[source],
            send_sem=s4.at[k], recv_sem=r4.at[source], device_id={"col": k}, device_id_type=MESH)

    def tile_rim_copy(k, source):
        return pltpu.make_async_remote_copy(
            src_ref=rim_out.at[k], dst_ref=rims.at[pl.ds(pl.multiple_of(16 * source, 16), 16), :],
            send_sem=s4h.at[k], recv_sem=r4h.at[source], device_id={"col": k}, device_id_type=MESH)

    own_tile = pltpu.make_async_copy(dp_out.at[col], tiles.at[col], r4.at[col])
    own_tile_rim = pltpu.make_async_copy(
        rim_out.at[col], rims.at[pl.ds(pl.multiple_of(16 * col, 16), 16), :], r4h.at[col])

    def back_y(c, carry):
        block = lax.rem(c + col // 2 + 1, NCOL // 2)
        cells = mm(flat[...], t1[:, pl.ds(pl.multiple_of(256 * block, 256), 256)]).astype(BF16)
        for m in range(2):
            k = 2 * block + m
            dp_out[k] = cells[:, 128 * m : 128 * m + 128]

            @pl.when(k != col)
            def _():
                tile_copy(k, col).start()

            @pl.when(k == col)
            def _():
                own_tile.start()

        return carry

    lax.fori_loop(0, NCOL // 2, back_y, 0)
    before = pick([(0, YB - 1)])
    after = pick([(1, 0)])
    for k in range(NCOL):
        edge = jnp.zeros((16, XB), F32)
        if k > 0:
            edge = edge + mm_nt(before, dp_out[k - 1])
        if k < NCOL - 1:
            edge = edge + mm_nt(after, dp_out[k + 1])
        rim_out[k] = jnp.concatenate([edge, jnp.zeros((16, 256 - XB), F32)], axis=1).astype(BF16)

        @pl.when(k != col)
        def _():
            tile_rim_copy(k, col).start()

        @pl.when(k == col)
        def _():
            own_tile_rim.start()

    own_tile.wait()
    own_tile_rim.wait()

    def finish_col(d, carry):
        k = lax.rem(col + d, NCOL)
        tile_copy(k, k).wait_recv()
        tile_rim_copy(k, k).wait_recv()
        line_copy(k, col).wait_send()
        line_rim_copy(k, col).wait_send()
        tile_copy(k, col).wait_send()
        tile_rim_copy(k, col).wait_send()
        return carry

    lax.fori_loop(1, NCOL, finish_col, 0)

    def finish_all(d, carry):
        other = lax.rem(me + d, everyone)
        half_copy(other, me).wait_send()
        back_copy(other // NCOL, lax.rem(other, NCOL), me).wait_send()
        return carry

    lax.fori_loop(1, everyone, finish_all, 0)


def transform(pred, halo, target, weight):
    along_y, rim, along_x = spectral_tables()
    vmem = pl.BlockSpec(memory_space=pltpu.VMEM)
    anywhere = pl.BlockSpec(memory_space=pl.ANY)
    dma = pltpu.SemaphoreType.DMA
    everyone = NROW * NCOL
    return pl.pallas_call(
        spectral_kernel,
        in_specs=[vmem, vmem] + [anywhere] * 5,
        out_specs=[vmem, vmem],
        out_shape=[
            jax.ShapeDtypeStruct((V, XB, YB), BF16),
            jax.ShapeDtypeStruct((V * 16, 256), BF16),
        ],
        scratch_shapes=[
            pltpu.VMEM((2 * NY, NY), BF16),
            pltpu.VMEM((2 * NY, 16 * NCOL), BF16),
            pltpu.VMEM((2 * NX, 2 * NX), BF16),
            pltpu.VMEM((V * QB, NX), F32),
            pltpu.VMEM((V * QB, NX), F32),
            pltpu.VMEM((256, NY), BF16),
            pltpu.VMEM((16 * NCOL, 256), BF16),
            pltpu.VMEM((NY, PACK), BF16),
            pltpu.VMEM((V * QB, 2 * NX), BF16),
            pltpu.VMEM((V * QB, 2 * NX), BF16),
            pltpu.VMEM((NROW, V * QB, PACK), BF16),
            pltpu.VMEM((NY, PACK), BF16),
            pltpu.VMEM((XB, 2 * NY), BF16),
            pltpu.VMEM((NCOL, XB, YB), BF16),
            pltpu.VMEM((NCOL, 16, 256), BF16),
            dma((5,)),
            dma((NCOL,)), dma((NCOL,)), dma((NCOL,)), dma((NCOL,)),
            dma((everyone,)), dma((everyone,)), dma((everyone,)), dma((everyone,)),
            dma((NCOL,)), dma((NCOL,)), dma((NCOL,)), dma((NCOL,)),
        ],
        compiler_params=pltpu.CompilerParams(
            collective_id=1, has_side_effects=True, vmem_limit_bytes=VMEM_LIMIT),
        name="transform",
    )(pred, halo, jnp.asarray(along_y), jnp.asarray(rim), jnp.asarray(along_x), target, weight)


def kgrad_kernel(tiles, rims, ft, shifted, grad, wide, mine, got_dp, got_row, got_col,
                 send, recv, s_dp, r_dp, s_row, r_row, s_col, r_col):
    dp = lax.axis_index("dp")
    row = lax.axis_index("row")
    col = lax.axis_index("col")
    up = lax.rem(row + NROW - 1, NROW)
    down = lax.rem(row + 1, NROW)
    axes = (("dp", dp, NDP), ("row", row, NROW), ("col", col, NCOL))

    barrier = pltpu.get_barrier_semaphore()
    for name, at, count in axes:
        for d in range(1, count):
            pl.semaphore_signal(barrier, inc=1, device_id={name: lax.rem(at + d, count)}, device_id_type=MESH)
    pl.semaphore_wait(barrier, NDP + NROW + NCOL - 3)

    columns = rims[...].astype(F32).T.astype(BF16)
    lane = lanes((XB, YB))
    for v in range(V):
        cells = tiles[v].astype(F32)
        edge = mm(columns[0:XB], pick([(16 * v, 0), (16 * v + 1, YB - 1)], rows=128))
        wide[pl.ds(v, XB, stride=32), :] = jnp.where(lane == YB - 1, edge, pltpu.roll(cells, YB - 1, 1))
        wide[pl.ds(8 + v, XB, stride=32), :] = cells
        wide[pl.ds(16 + v, XB, stride=32), :] = jnp.where(lane == 0, edge, pltpu.roll(cells, 1, 1))
        wide[pl.ds(24 + v, XB, stride=32), :] = jnp.zeros((XB, YB), F32)

    def narrow(g, carry):
        at = pl.multiple_of(512 * g, 512)
        shifted[pl.ds(32 + at, 512), :] = wide[pl.ds(at, 512), :].astype(BF16)
        return carry

    lax.fori_loop(0, GROUPS, narrow, 0)
    to_down = pltpu.make_async_remote_copy(
        src_ref=shifted.at[32 * XB : 32 * XB + 32], dst_ref=shifted.at[0:32],
        send_sem=send.at[0], recv_sem=recv.at[0], device_id={"row": down}, device_id_type=MESH)
    to_up = pltpu.make_async_remote_copy(
        src_ref=shifted.at[32:64], dst_ref=shifted.at[32 * XB + 32 : 32 * XB + 64],
        send_sem=send.at[1], recv_sem=recv.at[1], device_id={"row": up}, device_id_type=MESH)
    to_down.start()
    to_up.start()

    def gather(g, total):
        for pair in range(GROUP // 2):
            x = GROUP * g + 2 * pair
            at = pl.multiple_of(32 * x, 32)
            rows = jnp.concatenate([shifted[pl.ds(at, 96), :], shifted[pl.ds(at + 32, 96), :]], axis=1)
            cells = jnp.concatenate([ft[x], ft[x + 1]], axis=1)
            total = total + mm_nt(rows, cells)
        return total

    total = lax.fori_loop(1, GROUPS - 1, gather, jnp.zeros((96, C), F32))
    to_down.wait()
    to_up.wait()

    @pl.when(row == 0)
    def _():
        shifted[0:32] = jnp.zeros((32, YB), BF16)

    @pl.when(row == NROW - 1)
    def _():
        shifted[32 * XB + 32 : 32 * XB + 64] = jnp.zeros((32, YB), BF16)

    total = gather(0, total)
    total = gather(GROUPS - 1, total)
    total = jnp.concatenate([total, jnp.zeros((96, 128 - C), F32)], axis=1)
    mine[0] = jnp.concatenate([total[0:24], total[32:56], total[64:88]], axis=0)

    stages = ((axes[0], got_dp, s_dp, r_dp), (axes[1], got_row, s_row, r_row), (axes[2], got_col, s_col, r_col))
    for stage, ((name, at, count), got, s_sem, r_sem) in enumerate(stages):
        copies = [
            pltpu.make_async_remote_copy(
                src_ref=mine.at[stage], dst_ref=got.at[d - 1], send_sem=s_sem.at[d - 1], recv_sem=r_sem.at[d - 1],
                device_id={name: lax.rem(at + d, count)}, device_id_type=MESH)
            for d in range(1, count)
        ]
        for one in copies:
            one.start()
        total = mine[stage]
        for d in range(1, count):
            copies[d - 1].wait_recv()
        for source in range(count):
            term = mine[stage]
            for d in range(1, count):
                term = jnp.where(lax.rem(source + d, count) == at, got[d - 1], term)
            total = term if source == 0 else total + term
        if stage < 2:
            mine[stage + 1] = total
        else:
            grad[...] = total
        for one in copies:
            one.wait_send()


def kernel_gradient(tiles, rims, ft):
    vmem = pl.BlockSpec(memory_space=pltpu.VMEM)
    dma = pltpu.SemaphoreType.DMA
    return pl.pallas_call(
        kgrad_kernel,
        in_specs=[vmem] * 3,
        out_specs=[vmem] * 2,
        out_shape=[
            jax.ShapeDtypeStruct((32 * (XB + 2), YB), BF16),
            jax.ShapeDtypeStruct((72, 128), F32),
        ],
        scratch_shapes=[
            pltpu.VMEM((32 * XB, YB), F32),
            pltpu.VMEM((3, 72, 128), F32),
            pltpu.VMEM((NDP - 1, 72, 128), F32),
            pltpu.VMEM((NROW - 1, 72, 128), F32),
            pltpu.VMEM((NCOL - 1, 72, 128), F32),
            dma((2,)), dma((2,)),
            dma((NDP - 1,)), dma((NDP - 1,)),
            dma((NROW - 1,)), dma((NROW - 1,)),
            dma((NCOL - 1,)), dma((NCOL - 1,)),
        ],
        compiler_params=pltpu.CompilerParams(
            collective_id=2, has_side_effects=True, vmem_limit_bytes=VMEM_LIMIT),
        name="kernel_gradient",
    )(tiles, rims, ft)


def fgrad_kernel(shifted, w, out, turn):
    group = pl.program_id(0)
    for pair in range(GROUP // 2):
        at = pl.multiple_of(32 * (GROUP * group + 2 * pair), 32)
        rows = jnp.concatenate([shifted[pl.ds(at, 96), :], shifted[pl.ds(at + 32, 96), :]], axis=1)
        got = mm(w[...], rows)
        turn[pl.ds(2 * pair, C, stride=GROUP), :] = got[:, 0:YB]
        turn[pl.ds(2 * pair + 1, C, stride=GROUP), :] = got[:, YB : 2 * YB]
    out[...] = turn[...].reshape(C, GROUP, YB).astype(BF16)


def feature_gradient(shifted, weights):
    return pl.pallas_call(
        fgrad_kernel,
        grid=(GROUPS,),
        in_specs=[
            pl.BlockSpec((32 * (XB + 2), YB), lambda i: (0, 0)),
            pl.BlockSpec((C, 96), lambda i: (0, 0)),
        ],
        out_specs=pl.BlockSpec((C, GROUP, YB), lambda i: (0, i, 0)),
        out_shape=jax.ShapeDtypeStruct((C, XB, YB), BF16),
        scratch_shapes=[pltpu.VMEM((C * GROUP, YB), F32)],
        compiler_params=pltpu.CompilerParams(vmem_limit_bytes=VMEM_LIMIT),
        name="feature_gradient",
    )(shifted, weights)


def per_device(features, kernel, target_amp, spec_weight):
    by_tap = kernel.transpose(2, 3, 0, 1)
    w_forward = jnp.pad(by_tap.reshape(72, C), ((0, 8), (0, 0)))
    w_back = jnp.pad(by_tap[::-1], ((0, 0), (0, 1), (0, 0), (0, 0))).reshape(96, C).T
    ft, pred, halo = convolve(features.reshape(C, XB, YB), w_forward)
    tiles, rims = transform(pred, halo, target_amp.reshape(V * QB, NX), spec_weight.reshape(V * QB, NX))
    shifted, grad = kernel_gradient(tiles, rims, ft)
    feature_grad = feature_gradient(shifted, w_back).reshape(1, C, XB, YB)
    grad = grad[:, 0:C].reshape(3, 3, V, C)[::-1].transpose(2, 3, 0, 1)
    cells = NDP * NX * NY
    return grad / cells, feature_grad


def solution(mesh):
    return jax.shard_map(
        per_device,
        mesh=mesh,
        in_specs=(
            P("dp", None, "row", "col"),
            P(),
            P("dp", None, ("row", "col"), None),
            P(None, ("row", "col"), None),
        ),
        out_specs=(P(), P("dp", None, "row", "col")),
        check_vma=False,
    )
```

time: 563 us -> 111 us (0.20); the launches traced: 557 us -> 111 us
  matrix products: 266 us -> 0 us
  blocking collectives: 132 us -> 0 us
  local copies, waits for them, and re-layouts: 114 us -> 2.07 us
  Pallas kernels: 0 us -> 108 us
  starting transfers between devices: 25.1 us -> 0 us
  other arithmetic: 12.5 us -> 0.62 us
    dot_general x39 -> x0, matrix products: 266 us -> none  [the longest x9 68.2 us: per_device(): jnp.einsum('vc,svxy->scxy', kernel[:, :, first, second], window, preferre...]
    pallas_call x0 -> x4, Pallas kernels: none -> 108 us  [the longest x1 53.8 us: transform(): pl.pallas_call(spectral_kernel, in_specs=[vmem, vmem] + [anywhere] * 5, o...]
    all_to_all x4 -> x0, blocking collectives: 66.5 us -> none  [the longest x1 19.1 us: per_device(): lax.all_to_all(stacked, ('row', 'col'), split_axis=4, concat_axis=3, tile...]
    psum x1 -> x0, blocking collectives: 65.7 us -> none  [per_device(): summed = lax.psum(kernel_local, ('dp', 'row', 'col'))]
    unnamed x68 -> x4, local copies, waits for them, and re-layouts: 43.4 us -> 0.01 us
    all_to_all x7 -> x0, local copies, waits for them, and re-layouts: 35.9 us -> none  [the longest x3 20.3 us: per_device(): lax.all_to_all(backward, ('row', 'col'), split_axis=3, concat_axis=4, til...]
    ppermute x8 -> x0, starting transfers between devices: 25.1 us -> none  [the longest x4 16.4 us: extended(): lax.ppermute(tail, axis, [(i, (i + 1) % count) for i in range(ends)])]
    slice x6 -> x0, local copies, waits for them, and re-layouts: 15.3 us -> none  [the longest x3 10.5 us: extended(): lax.slice_in_dim(cells, cells.shape[dim] - width, cells.shape[dim], axis=...]
  transfers between devices with their start and end apart: 8 -> 0, of which waited for: 2 -> 0; matrix products, arithmetic and copies ran while one was open for 6% -> 0% of each run, Pallas kernels for 0% -> 0%
where the time goes in v1:
time: 111 us
  Pallas kernels  108 us (97%)
  local copies, waits for them, and re-layouts  2.07 us (2%)
    pallas_call x1, Pallas kernels, transform(): pl.pallas_call(spectral_kernel, in_specs=[vmem, vmem] + [anywhere] * 5, o...  53.8 us
    pallas_call x1, Pallas kernels, kernel_gradient(): pl.pallas_call(kgrad_kernel, in_specs=[vmem] * 3, out_specs=[vmem] * 2, o...  28.7 us
    pallas_call x1, Pallas kernels, convolve(): pl.pallas_call(conv_kernel, grid=(GROUPS,), in_specs=[pl.BlockSpec((C, GR...  16.2 us
    pallas_call x1, Pallas kernels, feature_gradient(): pl.pallas_call(fgrad_kernel, grid=(GROUPS,), in_specs=[pl.BlockSpec((32 *...  8.81 us

profile of v1, /device:TPU:1, one launch (start us, length us, event | category | flops | bytes accessed | tf_op | source)
XLA Modules:
  0.0 110.9 jit_solution(12642839407440183432)
XLA Ops:
  0.6 1.3 %pad.8.w = bf16[80,96]{1,0:T(8,128)(2,1)} pad(bf16[72,96]{1,0:T(8,128)(2,1)} %bitcast.19, bf16[]{:T(256)} %constant.10.clone.1), padding=0_8x0_0 | pad | bytes 29186 | tf_op jit(solution)/shard_map/jit(_pad)/pad | solution.py:618
  2.0 16.2 %convolve.1 = (bf16[192,96,128]{2,1,0:T(8,128)(2,1)}, bf16[8,192,128]{2,1,0:T(8,128)(2,1)}, bf16[8,16,256]{2,1,0:T(8,128)(2,1)}) custom-call(bf16[96,192,128]{2,1,0:T(8,128)(2,1)} %bitcast.14, bf16[80,96]{1,0:T(8,128)(2,1)} %pad.8.w), custom_call_target="tpu_custom_call" | custom-call | tf_op jit(solution)/shard_map/convolve/pallas_call | solution.py:154
  18.2 53.8 %transform.1 = (bf16[8,192,128]{2,1,0:T(8,128)(2,1)}, bf16[128,256]{1,0:T(8,128)(2,1)}) custom-call(bf16[8,192,128]{2,1,0:T(8,128)(2,1)} %get-tuple-element.9.pred, bf16[8,16,256]{2,1,0:T(8,128)(2,1)} %get-tuple-element.10.halo, bf16[2048,1024]{1,0:T(8,128)(2,1)} %constant.12.clone.t1_hbm, bf16[2048,128]{1,0:T(8,128)(2,1)} %constant.13.clone.rim_hbm, ...), custom_call_target="tpu_custom_call" | custom-call | tf_op jit(solution)/shard_map/transform/pallas_call | solution.py:434
  72.0 0.0 copy-start
  72.0 28.7 %kernel_gradient.1 = (bf16[6208,128]{1,0:T(8,128)(2,1)}, f32[72,128]{1,0:T(8,128)}) custom-call(bf16[8,192,128]{2,1,0:T(8,128)(2,1)} %get-tuple-element.11.tiles, bf16[128,256]{1,0:T(8,128)(2,1)} %get-tuple-element.12.rims, bf16[192,96,128]{2,1,0:T(8,128)(2,1)} %get-tuple-element.13.ft), custom_call_target="tpu_custom_call" | custom-call | tf_op jit(solution)/shard_map/kernel_gradient/pallas_call | solution.py:564
  100.7 0.0 copy-start.1
  100.8 0.0 copy-done
  100.8 0.7 copy.10
  101.5 8.8 %feature_gradient.1 = bf16[96,192,128]{2,1,0:T(8,128)(2,1)} custom-call(bf16[6208,128]{1,0:T(8,128)(2,1)} %get-tuple-element.15.shifted, bf16[96,96]{1,0:T(8,128)(2,1)} %bitcast.17), custom_call_target="tpu_custom_call" | custom-call | tf_op jit(solution)/shard_map/feature_gradient/pallas_call | solution.py:601
  110.3 0.0 copy-done.1
  110.3 0.6 multiply_bitcast_fusion
  (2 shorter events, 0.0 us)
Async XLA Ops:
  72.0 28.8 %copy-start = (bf16[8,96,3,3]{1,0,3,2:T(8,128)(2,1)S(1)}, bf16[8,96,3,3]{1,0,3,2:T(8,128)(2,1)}, u32[]{:S(2)}) copy-start(bf16[8,96,3,3]{1,0,3,2:T(8,128)(2,1)} %param.8) | copy-start | bytes 41476
  100.7 9.6 %copy-start.1 = (f32[72,128]{1,0:T(8,128)S(1)}, f32[72,128]{1,0:T(8,128)}, u32[]{:S(2)}) copy-start(f32[72,128]{1,0:T(8,128)} %get-tuple-element.14) | copy-start | bytes 110596

commit v2 on v0

v2 whole, which is shorter than its diff:
```python
import math

import jax
import jax.numpy as jnp
import ml_dtypes
import numpy as np
from jax import lax
from jax.experimental import pallas as pl
from jax.experimental.pallas import tpu as pltpu
from jax.sharding import PartitionSpec as P

MESH = pl.DeviceIdType.MESH
F32 = jnp.float32
BF16 = jnp.bfloat16
VMEM_LIMIT = 56 * 1024 * 1024

C = 96
V = 8
NX = 768
NY = 1024
NDP = 4
NROW = 4
NCOL = 8
XB = NX // NROW
YB = NY // NCOL
QB = NY // (NROW * NCOL)
HALF = NY // 2
GROUP = 16
GROUPS = XB // GROUP
PACK = 2 * XB


def dft_tables(length):
    index = np.arange(length, dtype=np.int64)
    product = (index[:, None] * index[None, :]) % length
    angles = product * (2.0 * math.pi / length)
    factor = 1.0 / math.sqrt(length)
    return np.cos(angles) * factor, np.sin(angles) * factor


def spectral_tables():
    cos_y, sin_y = dft_tables(NY)
    along_y = np.concatenate([cos_y[0:HALF], -sin_y[0:HALF]], axis=0)
    along_y[HALF] = cos_y[HALF]
    rim = np.zeros((NY, 16 * NCOL))
    for k in range(NCOL):
        if k > 0:
            rim[:, 16 * k] = along_y[:, YB * k - 1]
        if k < NCOL - 1:
            rim[:, 16 * k + 1] = along_y[:, YB * (k + 1)]
    cos_x, sin_x = dft_tables(NX)
    from_re = np.concatenate([cos_x, -sin_x], axis=0).T.reshape(NX // 64, 64, 2 * NX)
    from_im = np.concatenate([sin_x, cos_x], axis=0).T.reshape(NX // 64, 64, 2 * NX)
    along_x = np.stack([from_re, from_im], axis=1).reshape(2 * NX, 2 * NX)
    flip = np.zeros((NX, NX))
    flip[(NX - np.arange(NX)) % NX, np.arange(NX)] = 1.0
    bf16 = ml_dtypes.bfloat16
    return along_y.astype(bf16), rim.astype(bf16), along_x.astype(bf16), flip.astype(bf16)


def mm(a, b):
    return lax.dot_general(a, b, (((1,), (0,)), ((), ())), preferred_element_type=F32)


def mm_nt(a, b):
    return lax.dot_general(a, b, (((1,), (1,)), ((), ())), preferred_element_type=F32)


def lanes(shape):
    return lax.broadcasted_iota(jnp.int32, shape, len(shape) - 1)


def pick(row_lane_pairs, rows=16, width=128):
    r = lax.broadcasted_iota(jnp.int32, (rows, width), 0)
    c = lax.broadcasted_iota(jnp.int32, (rows, width), 1)
    hit = jnp.zeros((rows, width), F32)
    for row, lane in row_lane_pairs:
        hit = jnp.where((r == row) & (c == lane), 1.0, hit)
    return hit.astype(BF16)


def main_kernel(feat_hbm, w, t1_hbm, rim_hbm, t2_hbm, flip_hbm, targ_hbm, wt_hbm,
                shifted, grad,
                feat, ft, taps, pred, edges, halo, t1, t1rim, t2, flip, targ, wt,
                own_a, own_b, got_a, got_b, rows_out, rows_in, map_a, map_b,
                lines, rim_in, half, spec, grads, back, coef, flat, dp_out, rim_out, tiles, rims, columns,
                part, slots, mine, slots_col, total_ref,
                lf, load, sx, rx, sp, rp, s1, r1, s1h, r1h, s2, r2, s3, r3, s4, r4, s4h, r4h, sy, ry,
                sa, ra, sb, rb, sc, rc):
    dp = lax.axis_index("dp")
    row = lax.axis_index("row")
    col = lax.axis_index("col")
    me = NCOL * row + col
    up = lax.rem(row + NROW - 1, NROW)
    down = lax.rem(row + 1, NROW)
    low = me < 16
    block = jnp.where(low, me, 31 - me)
    vhalf = lax.rem(row, 2)
    group16 = NROW * dp + row

    def remote(src, dst, send, recv, where):
        return pltpu.make_async_remote_copy(
            src_ref=src, dst_ref=dst, send_sem=send, recv_sem=recv, device_id=where, device_id_type=MESH)

    def plane(j):
        return {"row": j // NCOL, "col": lax.rem(j, NCOL)}

    def rows(start, size):
        return pl.ds(pl.multiple_of(start, size), size)

    def feat_copy(g):
        at = rows(GROUP * g, GROUP)
        return pltpu.make_async_copy(feat_hbm.at[:, at], feat.at[:, at], lf.at[g])

    for i in range(GROUPS):
        feat_copy((i + GROUPS - 1) % GROUPS).start()
    loads = [pltpu.make_async_copy(src, dst, load.at[n]) for n, (src, dst) in enumerate(
        [(targ_hbm, targ), (wt_hbm, wt), (t1_hbm, t1), (rim_hbm, t1rim), (flip_hbm, flip), (t2_hbm, t2)])]
    loads[0].start()
    loads[1].start()

    barrier = pltpu.get_barrier_semaphore()

    def greet(d, carry):
        pl.semaphore_signal(barrier, inc=1, device_id=plane(lax.rem(me + d, 32)), device_id_type=MESH)
        return carry

    lax.fori_loop(1, 32, greet, 0)
    for d in range(1, NDP):
        for r in range(NROW):
            pl.semaphore_signal(barrier, inc=1, device_id={"dp": lax.rem(dp + d, NDP), "row": r}, device_id_type=MESH)

    def conv_group(i, carry):
        g = lax.rem(i + GROUPS - 1, GROUPS)
        feat_copy(g).wait()
        at = rows(GROUP * g, GROUP)
        ft[at] = jnp.swapaxes(feat[:, at, :], 0, 1)
        for pair in range(GROUP // 2):
            x = GROUP * g + 2 * pair
            got = mm(w[...], jnp.concatenate([ft[x], ft[x + 1]], axis=1))
            taps[1 + x] = got[0:72, 0:YB]
            taps[2 + x] = got[0:72, YB : 2 * YB]
        return carry

    lax.fori_loop(0, 3, conv_group, 0)
    pl.semaphore_wait(barrier, 31 + 12)
    to_down = remote(taps.at[XB, 0:24], taps.at[0, 0:24], sx.at[0], rx.at[0], {"row": down})
    to_up = remote(taps.at[1, 48:72], taps.at[XB + 1, 48:72], sx.at[1], rx.at[1], {"row": up})
    to_down.start()
    to_up.start()

    loads[0].wait()
    loads[1].wait()
    for one in loads[2:]:
        one.start()
    own_a[...] = (2.0 * wt[...]).astype(BF16)
    own_b[...] = (2.0 * wt[...] * targ[...]).astype(BF16)
    rows_out[...] = jnp.zeros((2, 16, NX), F32)
    for v in range(V):
        first = 2.0 * wt[QB * v : QB * v + 1, :]
        rows_out[v // 4, v % 4 : v % 4 + 1, :] = first
        rows_out[v // 4, 8 + v % 4 : 9 + v % 4, :] = first * targ[QB * v : QB * v + 1, :]
    partner = {"row": NROW - 1 - row, "col": NCOL - 1 - col}
    theirs = rows(128 * (1 - vhalf), 128)
    swap_a = remote(own_a.at[theirs], got_a, sp.at[0], rp.at[0], partner)
    swap_b = remote(own_b.at[theirs], got_b, sp.at[1], rp.at[1], partner)
    swap_a.start()
    swap_b.start()
    first_of = lax.rem(32 - me, 16)
    first_of = jnp.where(low, 0, first_of)
    row_low = remote(rows_out.at[first_of // 8], rows_in, sp.at[2], rp.at[2], plane(first_of))
    row_high = remote(rows_out.at[1 - first_of // 8], rows_in, sp.at[3], rp.at[2], plane(31 - first_of))

    @pl.when(me >= 16)
    def _():
        row_low.start()
        row_high.start()

    def line_copy(b, k, source):
        return remote(pred.at[k, 64 * b : 64 * b + 64],
                      lines.at[64 * b : 64 * b + 64, rows(YB * source, YB)],
                      s1.at[b, k], r1.at[b, source], {"col": k})

    def line_rim_copy(k, source):
        return remote(halo.at[k], rim_in.at[rows(16 * source, 16), :], s1h.at[k], r1h.at[source], {"col": k})

    def own_line(b):
        return pltpu.make_async_copy(pred.at[col, 64 * b : 64 * b + 64],
                                     lines.at[64 * b : 64 * b + 64, rows(YB * col, YB)], r1.at[b, col])

    own_rim = pltpu.make_async_copy(halo.at[col], rim_in.at[rows(16 * col, 16), :], r1h.at[col])
    lane128 = lanes((V * GROUP, YB))

    def combine(g, carry):
        x = GROUP * g
        total = (taps[pl.ds(x, GROUP), 0:24] + taps[pl.ds(x + 1, GROUP), 24:48]
                 + taps[pl.ds(x + 2, GROUP), 48:72])
        left = pltpu.roll(total[:, 0:8].reshape(V * GROUP, YB), 1, 1)
        mid = total[:, 8:16].reshape(V * GROUP, YB)
        right = pltpu.roll(total[:, 16:24].reshape(V * GROUP, YB), YB - 1, 1)
        cells = mid + jnp.where(lane128 == 0, 0.0, left) + jnp.where(lane128 == YB - 1, 0.0, right)
        edge = jnp.where(lane128 == 0, left, right)
        at = rows(x, GROUP)
        pred[:, at, :] = jnp.swapaxes(cells.reshape(GROUP, V, YB), 0, 1).astype(BF16)
        edges[:, at, :] = jnp.swapaxes(edge.reshape(GROUP, V, YB), 0, 1).astype(BF16)
        return carry

    def send_lines(b):
        def one(d, carry):
            line_copy(b, lax.rem(col + d, NCOL), col).start()
            return carry

        lax.fori_loop(1, NCOL, one, 0)
        own_line(b).start()

    lax.fori_loop(3, 6, conv_group, 0)
    to_down.wait()
    to_up.wait()

    @pl.when(row == 0)
    def _():
        taps[0, 0:24] = jnp.zeros((24, YB), F32)

    @pl.when(row == NROW - 1)
    def _():
        taps[XB + 1, 48:72] = jnp.zeros((24, YB), F32)

    lax.fori_loop(0, 4, combine, 0)
    send_lines(0)
    lax.fori_loop(6, 10, conv_group, 0)
    lax.fori_loop(4, 8, combine, 0)
    send_lines(1)
    lax.fori_loop(10, 12, conv_group, 0)
    lax.fori_loop(8, 12, combine, 0)
    send_lines(2)
    chosen = pick([(0, YB - 1), (1, 0)])
    for v in range(V):
        edge = mm_nt(chosen, edges[v])
        halo[v] = jnp.concatenate([edge, jnp.zeros((16, 256 - XB), F32)], axis=1).astype(BF16)

    def send_rims(d, carry):
        line_rim_copy(lax.rem(col + d, NCOL), col).start()
        return carry

    lax.fori_loop(1, NCOL, send_rims, 0)
    own_rim.start()

    for one in loads[2:]:
        one.wait()
    swap_a.wait_recv()
    swap_b.wait_recv()
    row_low.wait_recv()
    ours = rows(128 * vhalf, 128)
    r2d = lax.broadcasted_iota(jnp.int32, (128, 128), 0)
    c2d = lax.broadcasted_iota(jnp.int32, (128, 128), 1)
    mirror = jnp.where((r2d // QB == c2d // QB) & (lax.rem(r2d, QB) + lax.rem(c2d, QB) == QB), 1.0, 0.0).astype(BF16)
    sub16 = lax.broadcasted_iota(jnp.int32, (16, NX), 0)
    at_zero = jnp.where(block == 0, 1.0, 0.0)
    firsts = rows_in[...]
    firsts_half = (firsts * (1.0 - at_zero)).astype(BF16)
    own_w = 2.0 * wt[ours, :]
    for own, got, out, at, extra in (
            (own_w, got_a, map_a, 0, firsts),
            (own_w * targ[ours, :], got_b, map_b, 8, jnp.concatenate([firsts[8:16], firsts[0:8]], axis=0))):
        other = got[...].astype(F32)
        direct = jnp.where(low, own, other)
        raw = jnp.where(low, other, own).astype(BF16)
        mirrored = mm(mirror, raw) + mm(pick([(QB * v, at + v) for v in range(4)], rows=128, width=16), firsts_half)
        out[0:128, :] = direct + mm(mirrored.astype(BF16), flip[...])
        out[128:144, :] = jnp.where(sub16 < 4, extra, 0.0) * at_zero
    lines[XB:256, :] = jnp.zeros((256 - XB, NY), BF16)

    def wait_lines(d, carry):
        k = lax.rem(col + d, NCOL)
        for b in range(3):
            line_copy(b, k, k).wait_recv()
        line_rim_copy(k, k).wait_recv()
        return carry

    lax.fori_loop(1, NCOL, wait_lines, 0)
    for b in range(3):
        own_line(b).wait()
    own_rim.wait()

    def worker(b):
        return jnp.where(b // 8 == col // 4, b, 31 - b)

    def spec_at(r, i):
        return spec.at[rows(QB * i, QB), rows(PACK * r, PACK)]

    mine4 = lax.rem(col, 4)

    def half_copy(b):
        return remote(half.at[rows(QB * b, QB), :], spec_at(row, mine4),
                      s2.at[b], r2.at[NROW * row + mine4], plane(worker(b)))

    def half_arrival(r, i):
        return remote(half.at[0:QB, :], spec_at(r, i), s2.at[0], r2.at[NROW * r + i], {"row": r, "col": 4 * vhalf + i})

    own_half = pltpu.make_async_copy(
        half.at[rows(QB * block, QB), :], spec_at(row, mine4), r2.at[NROW * row + mine4])
    is_own = col // 4 == vhalf
    first64 = lanes((128, 128)) < 64

    def along_y(c, carry):
        chunk = lax.rem(c + block // 4 + 1, 4)
        q = rows(128 * chunk, 128)
        q_im = rows(HALF + 128 * chunk, 128)
        re = mm_nt(t1[q, :], lines[...]) + mm(t1rim[q, :], rim_in[...])
        im = mm_nt(t1[q_im, :], lines[...]) + mm(t1rim[q_im, :], rim_in[...])
        re0, re1 = re[:, 0:128], re[:, 128:256]
        im0, im1 = im[:, 0:128], im[:, 128:256]
        half[q, 0:128] = jnp.where(first64, re0, pltpu.roll(im0, 64, 1)).astype(BF16)
        half[q, 128:256] = jnp.where(first64, pltpu.roll(re0, 64, 1), im0).astype(BF16)
        half[q, 256:384] = jnp.where(first64, re1, pltpu.roll(im1, 64, 1)).astype(BF16)
        for m in range(4):
            b = 4 * chunk + m

            @pl.when(worker(b) != me)
            def _():
                half_copy(b).start()

            @pl.when(worker(b) == me)
            def _():
                own_half.start()

        return carry

    lax.fori_loop(0, 4, along_y, 0)

    def wait_half(n, carry):
        r = n // 4
        i = lax.rem(n, 4)
        own = (r == row) & (4 * vhalf + i == col)

        @pl.when(own)
        def _():
            own_half.wait()

        @pl.when(jnp.logical_not(own))
        def _():
            half_arrival(r, i).wait_recv()

        return carry

    lax.fori_loop(0, 16, wait_half, 0)

    lane_w = lanes((16, 2 * NX))
    sub_w = lax.broadcasted_iota(jnp.int32, (16, 2 * NX), 0)
    second_w = lax.rem(lane_w, 128) >= 64
    extra = jnp.zeros((16, 2 * NX), F32)
    for i in range(4):
        tile = spec[QB * i : QB * i + 16, :].astype(F32)
        moved = jnp.concatenate([pltpu.roll(tile[:, 128 * n : 128 * n + 128], 64, 1) for n in range(12)], axis=1)
        extra = jnp.where(jnp.logical_not(second_w) & (sub_w == i), moved[0:1, :], extra)
        spec[QB * i : QB * i + 16, :] = jnp.where(second_w & (sub_w == 0), tile * (1.0 - at_zero), tile).astype(BF16)
    spec[128:144, :] = (extra * at_zero).astype(BF16)

    def along_x(c, carry):
        p = rows(256 * c, 256)
        p_im = rows(NX + 256 * c, 256)
        re = mm(spec[...], t2[:, p])
        im = mm(spec[...], t2[:, p_im])
        factor = map_a[:, p] - map_b[:, p] / jnp.sqrt(re * re + im * im + 1.0)
        grads[:, p] = (factor * re).astype(BF16)
        grads[:, p_im] = (factor * im).astype(BF16)
        return carry

    lax.fori_loop(0, 3, along_x, 0)

    def back_copy(r, i):
        return remote(back.at[r, rows(QB * i, QB), :], coef.at[rows(QB * block, QB), :],
                      s3.at[NROW * r + i], r3.at[block], {"row": r, "col": 4 * vhalf + i})

    def back_arrival(b):
        return remote(back.at[0, 0:QB, :], coef.at[rows(QB * b, QB), :], s3.at[0], r3.at[b], plane(worker(b)))

    own_back = pltpu.make_async_copy(
        back.at[row, rows(QB * mine4, QB), :], coef.at[rows(QB * block, QB), :], r3.at[block])
    lane_b = lanes((16, PACK))
    sub_b = lax.broadcasted_iota(jnp.int32, (16, PACK), 0)
    second_b = (lax.rem(lane_b, 128) >= 64) & (sub_b == 0)

    def back_x(c, carry):
        r = lax.rem(row + 1 + c, NROW)
        got = mm_nt(grads[...], t2[rows(PACK * r, PACK), :])
        back[r] = got[0:128].astype(BF16)
        last = got[128:144]
        moved = jnp.concatenate([pltpu.roll(last[:, 128 * n : 128 * n + 128], 64, 1) for n in range(3)], axis=1)
        for i in range(4):
            tile = got[QB * i : QB * i + 16]
            fixed = tile * (1.0 - at_zero) + moved[i : i + 1, :] * at_zero
            back[r, QB * i : QB * i + 16] = jnp.where(second_b, fixed, tile).astype(BF16)
        for d in range(4):
            i = lax.rem(mine4 + d, 4)
            own = (r == row) & (4 * vhalf + i == col)

            @pl.when(own)
            def _():
                own_back.start()

            @pl.when(jnp.logical_not(own))
            def _():
                back_copy(r, i).start()

        return carry

    lax.fori_loop(0, NROW, back_x, 0)

    def wait_back(b, carry):
        @pl.when(worker(b) == me)
        def _():
            own_back.wait()

        @pl.when(worker(b) != me)
        def _():
            back_arrival(b).wait_recv()

        return carry

    lax.fori_loop(0, 16, wait_back, 0)

    for b in range(3):
        turned = coef[:, 128 * b : 128 * b + 128].T
        flat[64 * b : 64 * b + 64, 0:HALF] = turned[0:64]
        flat[64 * b : 64 * b + 64, HALF:NY] = turned[64:128]

    def tile_copy(k, source):
        return remote(dp_out.at[k], tiles.at[source], s4.at[k], r4.at[source], {"col": k})

    def tile_rim_copy(k, source):
        return remote(rim_out.at[k], rims.at[rows(16 * source, 16), :], s4h.at[k], r4h.at[source], {"col": k})

    own_tile = pltpu.make_async_copy(dp_out.at[col], tiles.at[col], r4.at[col])
    own_tile_rim = pltpu.make_async_copy(rim_out.at[col], rims.at[rows(16 * col, 16), :], r4h.at[col])

    def back_y(c, carry):
        two = lax.rem(c + col // 2 + 1, NCOL // 2)
        cells = mm(flat[...], t1[:, rows(256 * two, 256)]).astype(BF16)
        for m in range(2):
            k = 2 * two + m
            dp_out[k] = cells[:, 128 * m : 128 * m + 128]

            @pl.when(k != col)
            def _():
                tile_copy(k, col).start()

            @pl.when(k == col)
            def _():
                own_tile.start()

        return carry

    lax.fori_loop(0, NCOL // 2, back_y, 0)
    before = pick([(0, YB - 1)])
    after = pick([(1, 0)])
    for k in range(NCOL):
        edge = jnp.zeros((16, XB), F32)
        if k > 0:
            edge = edge + mm_nt(before, dp_out[k - 1])
        if k < NCOL - 1:
            edge = edge + mm_nt(after, dp_out[k + 1])
        rim_out[k] = jnp.concatenate([edge, jnp.zeros((16, 256 - XB), F32)], axis=1).astype(BF16)

        @pl.when(k != col)
        def _():
            tile_rim_copy(k, col).start()

        @pl.when(k == col)
        def _():
            own_tile_rim.start()

    own_tile.wait()
    own_tile_rim.wait()

    def wait_tiles(d, carry):
        k = lax.rem(col + d, NCOL)
        tile_copy(k, k).wait_recv()
        tile_rim_copy(k, k).wait_recv()
        return carry

    lax.fori_loop(1, NCOL, wait_tiles, 0)

    columns[...] = rims[...].astype(F32).T
    place = pick([(16 * v, 0) for v in range(V)] + [(16 * v + 1, YB - 1) for v in range(V)], rows=128)
    of_variable = (lax.broadcasted_iota(jnp.int32, (GROUP, V, YB), 2) // 16
                   == lax.broadcasted_iota(jnp.int32, (GROUP, V, YB), 1))

    def widen(g, carry):
        at = rows(GROUP * g, GROUP)
        cells = jnp.swapaxes(tiles[:, at, :].astype(F32), 0, 1).reshape(V * GROUP, YB)
        edge = jnp.where(of_variable, columns[at, :].reshape(GROUP, 1, YB), 0.0)
        edge = mm(edge.reshape(V * GROUP, YB).astype(BF16), place)
        later = jnp.where(lane128 == YB - 1, edge, pltpu.roll(cells, YB - 1, 1))
        sooner = jnp.where(lane128 == 0, edge, pltpu.roll(cells, 1, 1))
        wide = jnp.concatenate(
            [one.reshape(GROUP, V, YB) for one in (later, cells, sooner, jnp.zeros((V * GROUP, YB), F32))], axis=1)
        shifted[pl.ds(pl.multiple_of(32 + 512 * g, 32), 512), :] = wide.reshape(32 * GROUP, YB).astype(BF16)
        return carry

    lax.fori_loop(0, GROUPS, widen, 0)
    rim_down = remote(shifted.at[32 * XB : 32 * XB + 32], shifted.at[0:32], sy.at[0], ry.at[0], {"row": down})
    rim_up = remote(shifted.at[32:64], shifted.at[32 * XB + 32 : 32 * XB + 64], sy.at[1], ry.at[1], {"row": up})
    rim_down.start()
    rim_up.start()

    def gather(g, total):
        for pair in range(GROUP // 2):
            x = GROUP * g + 2 * pair
            at = pl.multiple_of(32 * x, 32)
            moved = jnp.concatenate([shifted[pl.ds(at, 96), :], shifted[pl.ds(at + 32, 96), :]], axis=1)
            total = total + mm_nt(jnp.concatenate([ft[x], ft[x + 1]], axis=1), moved)
        return total

    total = lax.fori_loop(1, GROUPS - 1, gather, jnp.zeros((C, 96), F32))
    rim_down.wait()
    rim_up.wait()

    @pl.when(row == 0)
    def _():
        shifted[0:32] = jnp.zeros((32, YB), BF16)

    @pl.when(row == NROW - 1)
    def _():
        shifted[32 * XB + 32 : 32 * XB + 64] = jnp.zeros((32, YB), BF16)

    total = gather(0, total)
    total = gather(GROUPS - 1, total)
    total = jnp.concatenate([total, jnp.zeros((C, 128 - 96), F32)], axis=1)
    part[0:C, :] = total
    part[C:128, :] = jnp.zeros((128 - C, 128), F32)

    def sixteen(n):
        return {"dp": n // NROW, "row": lax.rem(n, NROW)}

    def part_copy(n, source):
        return remote(part.at[rows(8 * n, 8)], slots.at[source], sa.at[n], ra.at[source], sixteen(n))

    def col_copy(k, source):
        return remote(mine, slots_col.at[source], sb.at[k], rb.at[source], {"col": k})

    def sum_copy(n, source):
        return remote(total_ref, grad.at[rows(8 * source, 8)], sc.at[n], rc.at[source], sixteen(n))

    def others16(act):
        def one(d, carry):
            act(lax.rem(group16 + d, 16))
            return carry

        lax.fori_loop(1, 16, one, 0)

    def others8(act):
        def one(d, carry):
            act(lax.rem(col + d, NCOL))
            return carry

        lax.fori_loop(1, NCOL, one, 0)

    others16(lambda n: part_copy(n, group16).start())
    slots[group16] = part[rows(8 * group16, 8), :]
    others16(lambda n: part_copy(n, n).wait_recv())
    partial = slots[0]
    for n in range(1, 16):
        partial = partial + slots[n]
    mine[...] = partial
    others8(lambda k: col_copy(k, col).start())
    slots_col[col] = partial
    others8(lambda k: col_copy(k, k).wait_recv())
    partial = slots_col[0]
    for n in range(1, NCOL):
        partial = partial + slots_col[n]
    total_ref[...] = partial
    others16(lambda n: sum_copy(n, group16).start())
    grad[rows(8 * group16, 8), :] = partial
    others16(lambda n: sum_copy(n, n).wait_recv())

    others16(lambda n: part_copy(n, group16).wait_send())
    others16(lambda n: sum_copy(n, group16).wait_send())
    swap_a.wait_send()
    swap_b.wait_send()

    @pl.when(me >= 16)
    def _():
        row_low.wait_send()
        row_high.wait_send()

    def finish_col(k):
        for b in range(3):
            line_copy(b, k, col).wait_send()
        line_rim_copy(k, col).wait_send()
        tile_copy(k, col).wait_send()
        tile_rim_copy(k, col).wait_send()
        col_copy(k, col).wait_send()

    others8(finish_col)

    def finish_half(b, carry):
        @pl.when(worker(b) != me)
        def _():
            half_copy(b).wait_send()

        r = b // 4
        i = lax.rem(b, 4)

        @pl.when(jnp.logical_not((r == row) & (4 * vhalf + i == col)))
        def _():
            back_copy(r, i).wait_send()

        return carry

    lax.fori_loop(0, 16, finish_half, 0)


def main_part(features, weights, target, weight):
    along_y, rim, along_x, flip = spectral_tables()
    vmem = pl.BlockSpec(memory_space=pltpu.VMEM)
    anywhere = pl.BlockSpec(memory_space=pl.ANY)
    dma = pltpu.SemaphoreType.DMA

    def b16(*shape):
        return pltpu.VMEM(shape, BF16)

    def f32(*shape):
        return pltpu.VMEM(shape, F32)

    return pl.pallas_call(
        main_kernel,
        in_specs=[anywhere, vmem] + [anywhere] * 6,
        out_specs=[vmem] * 2,
        out_shape=[
            jax.ShapeDtypeStruct((32 * (XB + 2), YB), BF16),
            jax.ShapeDtypeStruct((128, 128), F32),
        ],
        scratch_shapes=[
            b16(C, XB, YB), b16(XB, C, YB), f32(XB + 2, 72, YB), b16(V, XB, YB), b16(V, XB, YB), b16(V, 16, 256),
            b16(NY, NY), b16(NY, 16 * NCOL), b16(2 * NX, 2 * NX), b16(NX, NX), f32(V * QB, NX), f32(V * QB, NX),
            b16(V * QB, NX), b16(V * QB, NX), b16(128, NX), b16(128, NX), f32(2, 16, NX), f32(16, NX),
            f32(144, NX), f32(144, NX),
            b16(256, NY), b16(16 * NCOL, 256), b16(HALF, PACK), b16(144, 2 * NX), b16(144, 2 * NX),
            b16(NROW, 128, PACK), b16(HALF, PACK), b16(XB, NY), b16(NCOL, XB, YB), b16(NCOL, 16, 256),
            b16(V, XB, YB), b16(V * 16, 256), f32(256, 128),
            f32(128, 128), f32(16, 8, 128), f32(8, 128), f32(NCOL, 8, 128), f32(8, 128),
            dma((GROUPS,)), dma((6,)), dma((2,)), dma((2,)), dma((4,)), dma((3,)),
            dma((3, NCOL)), dma((3, NCOL)), dma((NCOL,)), dma((NCOL,)),
            dma((16,)), dma((16,)), dma((16,)), dma((16,)),
            dma((NCOL,)), dma((NCOL,)), dma((NCOL,)), dma((NCOL,)), dma((2,)), dma((2,)),
            dma((16,)), dma((16,)), dma((NCOL,)), dma((NCOL,)), dma((16,)), dma((16,)),
        ],
        compiler_params=pltpu.CompilerParams(
            collective_id=0, has_side_effects=True, vmem_limit_bytes=VMEM_LIMIT),
        name="main_part",
    )(features, weights, jnp.asarray(along_y), jnp.asarray(rim), jnp.asarray(along_x), jnp.asarray(flip),
      target, weight)


STEP = 96


def fgrad_kernel(shifted, w, out, turn):
    group = pl.program_id(0)

    def pair(n, carry):
        at = pl.multiple_of(32 * (STEP * group + 2 * n), 32)
        moved = jnp.concatenate([shifted[pl.ds(at, 96), :], shifted[pl.ds(at + 32, 96), :]], axis=1)
        got = mm(w[...], moved).astype(BF16)
        turn[2 * n] = got[:, 0:YB]
        turn[2 * n + 1] = got[:, YB : 2 * YB]
        return carry

    lax.fori_loop(0, STEP // 2, pair, 0, unroll=8)

    def turn_back(n, carry):
        at = pl.ds(pl.multiple_of(16 * n, 16), 16)
        out[:, at, :] = jnp.swapaxes(turn[at], 0, 1)
        return carry

    lax.fori_loop(0, STEP // 16, turn_back, 0)


def feature_gradient(shifted, weights):
    return pl.pallas_call(
        fgrad_kernel,
        grid=(XB // STEP,),
        in_specs=[
            pl.BlockSpec((32 * (XB + 2), YB), lambda i: (0, 0)),
            pl.BlockSpec((C, 96), lambda i: (0, 0)),
        ],
        out_specs=pl.BlockSpec((C, STEP, YB), lambda i: (0, i, 0)),
        out_shape=jax.ShapeDtypeStruct((C, XB, YB), BF16),
        scratch_shapes=[pltpu.VMEM((STEP, C, YB), BF16)],
        compiler_params=pltpu.CompilerParams(vmem_limit_bytes=VMEM_LIMIT),
        name="feature_gradient",
    )(shifted, weights)


def per_device(features, kernel, target_amp, spec_weight):
    by_tap = kernel.transpose(2, 3, 0, 1)
    w_forward = jnp.pad(by_tap.reshape(72, C), ((0, 8), (0, 0)))
    w_back = jnp.pad(by_tap[::-1], ((0, 0), (0, 1), (0, 0), (0, 0))).reshape(96, C).T
    shifted, grad = main_part(features.reshape(C, XB, YB), w_forward,
                              target_amp.reshape(V * QB, NX), spec_weight.reshape(V * QB, NX))
    feature_grad = feature_gradient(shifted, w_back).reshape(1, C, XB, YB)
    grad = grad[0:C, 0:96].reshape(C, 3, 4, V)[:, ::-1, 0:3].transpose(3, 0, 1, 2)
    cells = NDP * NX * NY
    return grad / cells, feature_grad


def solution(mesh):
    return jax.shard_map(
        per_device,
        mesh=mesh,
        in_specs=(
            P("dp", None, "row", "col"),
            P(),
            P("dp", None, ("row", "col"), None),
            P(None, ("row", "col"), None),
        ),
        out_specs=(P(), P("dp", None, "row", "col")),
        check_vma=False,
    )
```

time: 563 us -> 90.1 us (0.16); the launches traced: 557 us -> 89.7 us
  matrix products: 266 us -> 0 us
  blocking collectives: 132 us -> 0 us
  local copies, waits for them, and re-layouts: 114 us -> 3.66 us
  Pallas kernels: 0 us -> 84.8 us
  starting transfers between devices: 25.1 us -> 0 us
  other arithmetic: 12.5 us -> 0.62 us
    dot_general x39 -> x0, matrix products: 266 us -> none  [the longest x9 68.2 us: per_device(): jnp.einsum('vc,svxy->scxy', kernel[:, :, first, second], window, preferre...]
    pallas_call x0 -> x2, Pallas kernels: none -> 84.8 us  [the longest x1 77.4 us: main_part(): pl.pallas_call(main_kernel, in_specs=[anywhere, vmem] + [anywhere] * 6, o...]
    all_to_all x4 -> x0, blocking collectives: 66.5 us -> none  [the longest x1 19.1 us: per_device(): lax.all_to_all(stacked, ('row', 'col'), split_axis=4, concat_axis=3, tile...]
    psum x1 -> x0, blocking collectives: 65.7 us -> none  [per_device(): summed = lax.psum(kernel_local, ('dp', 'row', 'col'))]
    unnamed x68 -> x0, local copies, waits for them, and re-layouts: 43.4 us -> none
    all_to_all x7 -> x0, local copies, waits for them, and re-layouts: 35.9 us -> none  [the longest x3 20.3 us: per_device(): lax.all_to_all(backward, ('row', 'col'), split_axis=3, concat_axis=4, til...]
    ppermute x8 -> x0, starting transfers between devices: 25.1 us -> none  [the longest x4 16.4 us: extended(): lax.ppermute(tail, axis, [(i, (i + 1) % count) for i in range(ends)])]
    slice x6 -> x3, local copies, waits for them, and re-layouts: 15.3 us -> 0.89 us  [per_device(): grad[0:C, 0:96].reshape(C, 3, 4, V)[:, ::-1, 0:3].transpose(3, 0, 1, 2)]
  transfers between devices with their start and end apart: 8 -> 0, of which waited for: 2 -> 0; matrix products, arithmetic and copies ran while one was open for 6% -> 0% of each run, Pallas kernels for 0% -> 0%
where the time goes in v2:
time: 90.1 us; the launch traced here: 89.7 us
  Pallas kernels  84.8 us (94%)
  local copies, waits for them, and re-layouts  3.66 us (4%)
    pallas_call x1, Pallas kernels, main_part(): pl.pallas_call(main_kernel, in_specs=[anywhere, vmem] + [anywhere] * 6, o...  77.4 us
    pallas_call x1, Pallas kernels, feature_gradient(): pl.pallas_call(fgrad_kernel, grid=(XB // STEP,), in_specs=[pl.BlockSpec((...  7.36 us

profile of v2, /device:TPU:1, one launch (start us, length us, event | category | flops | bytes accessed | tf_op | source)
XLA Modules:
  0.0 89.7 jit_solution(9193973728469550457)
XLA Ops:
  0.6 0.7 rev.7
  1.4 0.7 copy.13
  2.1 1.3 %pad.8.w = bf16[80,96]{1,0:T(8,128)(2,1)} pad(bf16[72,96]{1,0:T(8,128)(2,1)} %bitcast.20, bf16[]{:T(256)} %constant.12.clone.1), padding=0_8x0_0 | pad | bytes 29186 | tf_op jit(solution)/shard_map/jit(_pad)/pad | solution.py:698
  3.4 77.4 %main_part.1 = (bf16[6208,128]{1,0:T(8,128)(2,1)}, f32[128,128]{1,0:T(8,128)}) custom-call(bf16[96,192,128]{2,1,0:T(8,128)(2,1)} %bitcast.12, bf16[80,96]{1,0:T(8,128)(2,1)} %pad.8.w, bf16[1024,1024]{1,0:T(8,128)(2,1)} %constant.14.clone.t1_hbm, bf16[1024,128]{1,0:T(8,128)(2,1)} %constant.15.clone.rim_hbm, bf16[1536,1536]{1,0:T(8,128)(2,1)} %constant.16.clone.t2_hbm, ...), custom_call_target="tpu_custom_call" | custom-call | tf_op jit(solution)/shard_map/main_part/pallas_call | solution.py:626
  80.8 0.8 slice.6
  81.6 0.1 copy.12
  81.7 0.6 multiply_bitcast_fusion
  82.4 7.4 %feature_gradient.1 = bf16[96,192,128]{2,1,0:T(8,128)(2,1)} custom-call(bf16[6208,128]{1,0:T(8,128)(2,1)} %get-tuple-element.5.shifted, bf16[96,96]{1,0:T(8,128)(2,1)} %bitcast.17), custom_call_target="tpu_custom_call" | custom-call | tf_op jit(solution)/shard_map/feature_gradient/pallas_call | solution.py:681
  (2 shorter events, 0.0 us)
